TPU v7x, 32 devices: a whole 2x2x4 slice. The times are simulated.
32 devices in a mesh: dp: 8 (over z, y), sp: 4 (over x, core).
Axes of the slice: x: 2, y: 2, z: 4, core: 2. Of those that a mesh axis runs over, the one named last changes fastest.
Arguments:
- queries: bfloat16 [4096, 2560], P(('dp', 'sp')), may hold values from -80 to 80
- key_rows: bfloat16 [4096, 2560], P(('dp', 'sp')), may hold values from -5 to 5
- value_rows: bfloat16 [4096, 2560], P(('dp', 'sp')), may hold values from -6 to 6
- cotangent: bfloat16 [4096, 2560], P(('dp', 'sp')), may hold values from -6 to 6
- lengths: int32 [8], replicated, may hold values from 1 to 512, 2560 in all
- sample_plan: int32 [8], replicated, may hold values from 0 to 7, each once
- guide_bins: int32 [8], replicated, may hold values from 0 to 7
- guide_table: float32 [8, 20], replicated, may hold values from 0.5 to 2
- block_source: int32 [1024], replicated, may hold values from 0 to 1023, as said below
Outputs:
- attn_out: bfloat16 [4096, 2560], P(('dp', 'sp'))
- grad_queries: bfloat16 [4096, 2560], P(('dp', 'sp'))
- grad_keys: bfloat16 [4096, 2560], P(('dp', 'sp'))
- grad_values: bfloat16 [4096, 2560], P(('dp', 'sp'))
Inputs may be any that keep to these rules, and one draw needn't show every extreme that they name: `lengths`: the longest sample has exactly 512 tokens. `sample_plan`: every group takes exactly one sample. `block_source`: a permutation; the 32 row blocks of the group order that one device holds come one from each device's loader rows, and each device's 32 loader row blocks go one to each device.
All inputs are finite; a program needn't handle non-finite values.
Results may differ from a plain program's by a relative error of at most 0.009.
Values may be sent and summed in bfloat16 or wider, within the bound.
A program may use at most 64 MiB of HBM per device.

v0:
```python
import jax
import jax.numpy as jnp
from jax import lax
from jax.sharding import PartitionSpec as P

HEADS = 20
HD = 128


def head_pass(query_head, key_head, value_head, grad_head, query_live, key_live):
    scores = jnp.dot(query_head, key_head.T, preferred_element_type=jnp.float32) * HD ** (-0.5)
    masked = jnp.where(key_live[None, :], scores, -1e30)
    top_score = jnp.max(masked, axis=1, keepdims=True)
    shifted_exp = jnp.where(key_live[None, :], jnp.exp(masked - top_score), 0.0)
    row_total = jnp.sum(shifted_exp, axis=1, keepdims=True)
    attend = jnp.where(query_live[:, None], shifted_exp / row_total, 0.0)
    attend_bf = attend.astype(jnp.bfloat16)
    output = jnp.dot(attend_bf, value_head, preferred_element_type=jnp.float32)
    grad_attend = jnp.dot(grad_head, value_head.T, preferred_element_type=jnp.float32)
    row_dot = jnp.sum(grad_head.astype(jnp.float32) * output, axis=1, keepdims=True)
    grad_scores = (attend * (grad_attend - row_dot) * HD ** (-0.5)).astype(jnp.bfloat16)
    grad_query = jnp.dot(grad_scores, key_head, preferred_element_type=jnp.float32)
    grad_key = jnp.dot(grad_scores.T, query_head, preferred_element_type=jnp.float32)
    grad_value = jnp.dot(attend_bf.T, grad_head, preferred_element_type=jnp.float32)
    return (output, grad_query, grad_key, grad_value)


def head_stack(query_part, key_part, value_part, grad_part, query_live, key_live):

    def one_head(head_items):
        return head_pass(
            head_items[0], head_items[1], head_items[2], head_items[3], query_live, key_live
        )

    stacked = tuple(
        (jnp.moveaxis(source, 1, 0) for source in (query_part, key_part, value_part, grad_part))
    )
    return lax.map(one_head, stacked)


def dispatch(first, second, third):
    return (
        lax.all_to_all(first, ("dp", "sp"), split_axis=0, concat_axis=0, tiled=True),
        lax.all_to_all(second, ("dp", "sp"), split_axis=0, concat_axis=0, tiled=True),
        lax.all_to_all(third, ("dp", "sp"), split_axis=0, concat_axis=0, tiled=True),
    )


def send_back(first, second, third):
    return (
        lax.all_to_all(first, ("dp", "sp"), split_axis=0, concat_axis=0, tiled=True),
        lax.all_to_all(second, ("dp", "sp"), split_axis=0, concat_axis=0, tiled=True),
        lax.all_to_all(third, ("dp", "sp"), split_axis=0, concat_axis=0, tiled=True),
    )


def per_device(
    queries,
    key_rows,
    value_rows,
    cotangent,
    lengths,
    sample_plan,
    guide_bins,
    guide_table,
    block_source,
):
    n_dp = lax.axis_size("dp")
    n_sp = lax.axis_size("sp")
    loaders = n_dp * n_sp
    tok_rows = queries.shape[0]
    row_width = queries.shape[1]
    block_rows = tok_rows // loaders
    device_index = lax.axis_index("dp") * n_sp + lax.axis_index("sp")
    table = block_source.reshape(loaders, loaders)
    sources = table[device_index] // loaders
    send_slot = jnp.sum(jnp.where(table // loaders == device_index, table % loaders, 0), axis=1)
    slot_index = jnp.arange(loaders, dtype=jnp.int32)
    back_slot = jnp.sum(
        jnp.where(sources[None, :] == slot_index[:, None], slot_index[None, :], 0), axis=1
    )
    loader_slot = jnp.sum(
        jnp.where(send_slot[None, :] == slot_index[:, None], slot_index[None, :], 0), axis=1
    )

    def as_blocks(source, order):
        return source.reshape(loaders, block_rows, row_width)[order]

    recv_query, recv_key, recv_value = dispatch(
        as_blocks(queries, send_slot),
        as_blocks(key_rows, send_slot),
        as_blocks(value_rows, send_slot),
    )
    query_own = recv_query[sources].reshape(tok_rows, HEADS, HD)
    key_own = recv_key[sources].reshape(tok_rows, HEADS, HD)
    value_own = recv_value[sources].reshape(tok_rows, HEADS, HD)
    group_index = lax.axis_index("dp")
    picked = sample_plan == group_index
    group_len = jnp.sum(jnp.where(picked, lengths, 0))
    group_bin = jnp.sum(jnp.where(picked, guide_bins, 0))
    bin_match = jnp.arange(guide_table.shape[0], dtype=jnp.int32) == group_bin
    head_gate = jnp.sum(jnp.where(bin_match[:, None], guide_table, 0.0), axis=0)
    grad_own = (
        head_gate[None, :, None] * cotangent.reshape(tok_rows, HEADS, HD).astype(jnp.float32)
    ).astype(jnp.bfloat16)
    heads_dev = HEADS // n_sp
    split_shape = (tok_rows, n_sp, heads_dev, HD)
    group_items = (
        lax.all_to_all(
            query_own.reshape(split_shape), "sp", split_axis=1, concat_axis=0, tiled=True
        ),
        lax.all_to_all(key_own.reshape(split_shape), "sp", split_axis=1, concat_axis=0, tiled=True),
        lax.all_to_all(
            value_own.reshape(split_shape), "sp", split_axis=1, concat_axis=0, tiled=True
        ),
        lax.all_to_all(
            grad_own.reshape(split_shape), "sp", split_axis=1, concat_axis=0, tiled=True
        ),
    )
    flat_items = tuple((item[:, 0] for item in group_items))
    live_rows = jnp.arange(flat_items[0].shape[0], dtype=jnp.int32) < group_len
    results = head_stack(
        flat_items[0], flat_items[1], flat_items[2], flat_items[3], live_rows, live_rows
    )
    out_heads, gq_heads, gk_heads, gv_heads = tuple(
        (jnp.moveaxis(result, 0, 1)[:, None].astype(jnp.bfloat16) for result in results)
    )
    back_rows = (
        lax.all_to_all(out_heads, "sp", split_axis=0, concat_axis=1, tiled=True),
        lax.all_to_all(gq_heads, "sp", split_axis=0, concat_axis=1, tiled=True),
        lax.all_to_all(gk_heads, "sp", split_axis=0, concat_axis=1, tiled=True),
        lax.all_to_all(gv_heads, "sp", split_axis=0, concat_axis=1, tiled=True),
    )
    out_bf, grad_q_own, grad_k_own, grad_v_own = tuple(
        (part.reshape(tok_rows, HEADS, HD) for part in back_rows)
    )
    attn_out = (
        (head_gate[None, :, None] * lax.optimization_barrier(out_bf).astype(jnp.float32))
        .astype(jnp.bfloat16)
        .reshape(tok_rows, row_width)
    )
    back_query, back_key, back_value = send_back(
        as_blocks(grad_q_own, back_slot),
        as_blocks(grad_k_own, back_slot),
        as_blocks(grad_v_own, back_slot),
    )
    grad_queries = back_query[loader_slot].reshape(tok_rows, row_width)
    grad_keys = back_key[loader_slot].reshape(tok_rows, row_width)
    grad_values = back_value[loader_slot].reshape(tok_rows, row_width)
    return (attn_out, grad_queries, grad_keys, grad_values)


def solution(mesh):
    placed = (
        P(("dp", "sp"), None),
        P(("dp", "sp"), None),
        P(("dp", "sp"), None),
        P(("dp", "sp"), None),
        P(),
        P(),
        P(),
        P(),
        P(),
    )
    return jax.shard_map(
        per_device,
        mesh=mesh,
        in_specs=placed,
        out_specs=(
            P(("dp", "sp"), None),
            P(("dp", "sp"), None),
            P(("dp", "sp"), None),
            P(("dp", "sp"), None),
        ),
        check_vma=False,
    )
```

profile of v0, /device:TPU:0, one launch (start us, length us, event | category | flops | bytes accessed | tf_op | source)
XLA Modules:
  0.0 309.7 jit_solution(6560074655742271941)
XLA Ops:
  6.0 4.2 %all-to-all-start.6 = ((bf16[128,4,5,128]{0,3,2,1:T(8,128)(2,1)}), bf16[128,4,5,128]{0,3,2,1:T(8,128)(2,1)S(1)}, u32[]{:S(2)}, u32[]{:S(2)}) async-start(bf16[128,4,5,128]{0,3,2,1:T(8,128)(2,1)} %fusion.32), calls=%async_computation.6 | async-start | bytes 1310720 | tf_op jit(solution)/shard_map/all_to_all | solution.py:116
  12.5 8.0 %all-to-all-done.6 = bf16[128,4,5,128]{0,3,2,1:T(8,128)(2,1)S(1)} async-done(((bf16[128,4,5,128]{0,3,2,1:T(8,128)(2,1)}), bf16[128,4,5,128]{0,3,2,1:T(8,128)(2,1)S(1)}, u32[]{:S(2)}, u32[]{:S(2)}) %all-to-all-start.6) | async-done | bytes 655392 | tf_op jit(solution)/shard_map/all_to_all | solution.py:116
  20.4 5.6 %all-to-all-start = ((bf16[32,4,2560]{2,1,0:T(4,128)(2,1)}), bf16[32,4,2560]{2,1,0:T(4,128)(2,1)S(1)}, u32[]{:S(2)}, u32[]{:S(2)}) async-start(bf16[32,4,2560]{2,1,0:T(4,128)(2,1)} %gather_fusion), calls=%async_computation | async-start | bytes 1310720 | tf_op jit(solution)/shard_map/all_to_all | solution.py:43
  28.1 15.8 %all-to-all-done = bf16[32,4,2560]{2,1,0:T(4,128)(2,1)S(1)} async-done(((bf16[32,4,2560]{2,1,0:T(4,128)(2,1)}), bf16[32,4,2560]{2,1,0:T(4,128)(2,1)S(1)}, u32[]{:S(2)}, u32[]{:S(2)}) %all-to-all-start) | async-done | bytes 655392 | tf_op jit(solution)/shard_map/all_to_all | solution.py:43
  44.0 3.5 %all-to-all-start.2 = ((bf16[32,4,2560]{2,1,0:T(4,128)(2,1)}), bf16[32,4,2560]{2,1,0:T(4,128)(2,1)S(1)}, u32[]{:S(2)}, u32[]{:S(2)}) async-start(bf16[32,4,2560]{2,1,0:T(4,128)(2,1)} %gather_fusion.2), calls=%async_computation.2 | async-start | bytes 1310720 | tf_op jit(solution)/shard_map/all_to_all | solution.py:44
  49.5 15.8 %all-to-all-done.2 = bf16[32,4,2560]{2,1,0:T(4,128)(2,1)S(1)} async-done(((bf16[32,4,2560]{2,1,0:T(4,128)(2,1)}), bf16[32,4,2560]{2,1,0:T(4,128)(2,1)S(1)}, u32[]{:S(2)}, u32[]{:S(2)}) %all-to-all-start.2) | async-done | bytes 655392 | tf_op jit(solution)/shard_map/all_to_all | solution.py:44
  65.4 3.5 %all-to-all-start.4 = ((bf16[32,4,2560]{2,1,0:T(4,128)(2,1)}), bf16[32,4,2560]{2,1,0:T(4,128)(2,1)S(1)}, u32[]{:S(2)}, u32[]{:S(2)}) async-start(bf16[32,4,2560]{2,1,0:T(4,128)(2,1)} %gather_fusion.4), calls=%async_computation.4 | async-start | bytes 1310720 | tf_op jit(solution)/shard_map/all_to_all | solution.py:45
  70.9 1.9 reshape_reshape.18
  73.9 12.9 %all-to-all-done.4 = bf16[32,4,2560]{2,1,0:T(4,128)(2,1)S(1)} async-done(((bf16[32,4,2560]{2,1,0:T(4,128)(2,1)}), bf16[32,4,2560]{2,1,0:T(4,128)(2,1)S(1)}, u32[]{:S(2)}, u32[]{:S(2)}) %all-to-all-start.4) | async-done | bytes 655392 | tf_op jit(solution)/shard_map/all_to_all | solution.py:45
  86.8 4.2 %all-to-all-start.1 = ((bf16[128,4,5,128]{3,0,2,1:T(8,128)(2,1)}), bf16[128,4,5,128]{3,0,2,1:T(8,128)(2,1)}, u32[]{:S(2)}, u32[]{:S(2)}) async-start(bf16[128,4,5,128]{3,0,2,1:T(8,128)(2,1)} %copy.72), calls=%async_computation.1 | async-start | bytes 1310720 | tf_op jit(solution)/shard_map/all_to_all | solution.py:109
  93.9 7.4 %all-to-all-done.1 = bf16[128,4,5,128]{3,0,2,1:T(8,128)(2,1)} async-done(((bf16[128,4,5,128]{3,0,2,1:T(8,128)(2,1)}), bf16[128,4,5,128]{3,0,2,1:T(8,128)(2,1)}, u32[]{:S(2)}, u32[]{:S(2)}) %all-to-all-start.1) | async-done | bytes 655392 | tf_op jit(solution)/shard_map/all_to_all | solution.py:109
  101.3 3.5 %all-to-all-start.3 = ((bf16[128,4,5,128]{3,0,2,1:T(8,128)(2,1)}), bf16[128,4,5,128]{3,0,2,1:T(8,128)(2,1)S(1)}, u32[]{:S(2)}, u32[]{:S(2)}) async-start(bf16[128,4,5,128]{3,0,2,1:T(8,128)(2,1)} %copy.74), calls=%async_computation.3 | async-start | bytes 1310720 | tf_op jit(solution)/shard_map/all_to_all | solution.py:112
  107.7 7.3 %all-to-all-done.3 = bf16[128,4,5,128]{3,0,2,1:T(8,128)(2,1)S(1)} async-done(((bf16[128,4,5,128]{3,0,2,1:T(8,128)(2,1)}), bf16[128,4,5,128]{3,0,2,1:T(8,128)(2,1)S(1)}, u32[]{:S(2)}, u32[]{:S(2)}) %all-to-all-start.3) | async-done | bytes 655392 | tf_op jit(solution)/shard_map/all_to_all | solution.py:112
  115.0 3.7 %all-to-all-start.5 = ((bf16[128,4,5,128]{3,0,2,1:T(8,128)(2,1)}), bf16[128,4,5,128]{3,0,2,1:T(8,128)(2,1)S(1)}, u32[]{:S(2)}, u32[]{:S(2)}) async-start(bf16[128,4,5,128]{3,0,2,1:T(8,128)(2,1)} %copy.76), calls=%async_computation.5 | async-start | bytes 1310720 | tf_op jit(solution)/shard_map/all_to_all | solution.py:113
  120.3 8.5 %all-to-all-done.5 = bf16[128,4,5,128]{3,0,2,1:T(8,128)(2,1)S(1)} async-done(((bf16[128,4,5,128]{3,0,2,1:T(8,128)(2,1)}), bf16[128,4,5,128]{3,0,2,1:T(8,128)(2,1)S(1)}, u32[]{:S(2)}, u32[]{:S(2)}) %all-to-all-start.5) | async-done | bytes 655392 | tf_op jit(solution)/shard_map/all_to_all | solution.py:113
  129.6 38.5 %while.17 = (s32[]{:T(128)}, bf16[5,512,128]{2,1,0:T(8,128)(2,1)}, bf16[5,512,128]{2,1,0:T(8,128)(2,1)}, bf16[5,512,128]{2,1,0:T(8,128)(2,1)}, bf16[5,512,128]{2...) while((s32[]{:T(128)}, bf16[5,512,128]{2,1,0:T(8,128)(2,1)}, ...), condition=%wide.region_8.9_spmd.clone, body=%wide.region_4.8_spmd.clone.sunk | while | flops 409205760 | bytes 9993861 | solution.py:38
  168.1 2.5 copy.85
  170.6 3.6 %all-to-all-start.7 = ((bf16[512,1,5,128]{3,2,1,0:T(8,128)(2,1)}), bf16[512,1,5,128]{3,2,1,0:T(8,128)(2,1)S(1)}, u32[]{:S(2)}, u32[]{:S(2)}) async-start(bf16[512,1,5,128]{3,2,1,0:T(8,128)(2,1)} %copy.85), calls=%async_computation.7 | async-start | bytes 2097152 | tf_op jit(solution)/shard_map/all_to_all | solution.py:129
  175.8 12.9 %all-to-all-done.7 = bf16[512,1,5,128]{3,2,1,0:T(8,128)(2,1)S(1)} async-done(((bf16[512,1,5,128]{3,2,1,0:T(8,128)(2,1)}), bf16[512,1,5,128]{3,2,1,0:T(8,128)(2,1)S(1)}, u32[]{:S(2)}, u32[]{:S(2)}) %all-to-all-start.7) | async-done | bytes 655392 | tf_op jit(solution)/shard_map/all_to_all | solution.py:129
  189.7 3.5 %all-to-all-start.12 = ((bf16[512,1,5,128]{3,2,1,0:T(8,128)(2,1)}), bf16[512,1,5,128]{3,2,1,0:T(8,128)(2,1)S(1)}, u32[]{:S(2)}, u32[]{:S(2)}) async-start(bf16[512,1,5,128]{3,2,1,0:T(8,128)(2,1)} %copy.93), calls=%async_computation.12 | async-start | bytes 2097152 | tf_op jit(solution)/shard_map/all_to_all | solution.py:132
  194.7 13.0 %all-to-all-done.12 = bf16[512,1,5,128]{3,2,1,0:T(8,128)(2,1)S(1)} async-done(((bf16[512,1,5,128]{3,2,1,0:T(8,128)(2,1)}), bf16[512,1,5,128]{3,2,1,0:T(8,128)(2,1)S(1)}, u32[]{:S(2)}, u32[]{:S(2)}) %all-to-all-start.12) | async-done | bytes 655392 | tf_op jit(solution)/shard_map/all_to_all | solution.py:132
  207.7 3.5 %all-to-all-start.8 = ((bf16[512,1,5,128]{3,2,1,0:T(8,128)(2,1)}), bf16[512,1,5,128]{3,2,1,0:T(8,128)(2,1)S(1)}, u32[]{:S(2)}, u32[]{:S(2)}) async-start(bf16[512,1,5,128]{3,2,1,0:T(8,128)(2,1)} %copy.89), calls=%async_computation.8 | async-start | bytes 2097152 | tf_op jit(solution)/shard_map/all_to_all | solution.py:130
  212.7 12.9 %all-to-all-done.8 = bf16[512,1,5,128]{3,2,1,0:T(8,128)(2,1)S(1)} async-done(((bf16[512,1,5,128]{3,2,1,0:T(8,128)(2,1)}), bf16[512,1,5,128]{3,2,1,0:T(8,128)(2,1)S(1)}, u32[]{:S(2)}, u32[]{:S(2)}) %all-to-all-start.8) | async-done | bytes 655392 | tf_op jit(solution)/shard_map/all_to_all | solution.py:130
  225.6 3.5 %all-to-all-start.10 = ((bf16[512,1,5,128]{3,2,1,0:T(8,128)(2,1)}), bf16[512,1,5,128]{3,2,1,0:T(8,128)(2,1)S(1)}, u32[]{:S(2)}, u32[]{:S(2)}) async-start(bf16[512,1,5,128]{3,2,1,0:T(8,128)(2,1)} %copy.91), calls=%async_computation.10 | async-start | bytes 2097152 | tf_op jit(solution)/shard_map/all_to_all | solution.py:131
  234.2 9.3 %all-to-all-done.10 = bf16[512,1,5,128]{3,2,1,0:T(8,128)(2,1)S(1)} async-done(((bf16[512,1,5,128]{3,2,1,0:T(8,128)(2,1)}), bf16[512,1,5,128]{3,2,1,0:T(8,128)(2,1)S(1)}, u32[]{:S(2)}, u32[]{:S(2)}) %all-to-all-start.10) | async-done | bytes 655392 | tf_op jit(solution)/shard_map/all_to_all | solution.py:131
  243.6 3.3 %all-to-all-start.13 = ((bf16[32,4,2560]{2,1,0:T(4,128)(2,1)}), bf16[32,4,2560]{2,1,0:T(4,128)(2,1)}, u32[]{:S(2)}, u32[]{:S(2)}) async-start(bf16[32,4,2560]{2,1,0:T(4,128)(2,1)} %gather_fusion.10), calls=%async_computation.13 | async-start | bytes 1310720 | tf_op jit(solution)/shard_map/all_to_all | solution.py:53
  249.4 15.4 %all-to-all-done.13 = bf16[32,4,2560]{2,1,0:T(4,128)(2,1)} async-done(((bf16[32,4,2560]{2,1,0:T(4,128)(2,1)}), bf16[32,4,2560]{2,1,0:T(4,128)(2,1)}, u32[]{:S(2)}, u32[]{:S(2)}) %all-to-all-start.13) | async-done | bytes 655392 | tf_op jit(solution)/shard_map/all_to_all | solution.py:53
  264.8 3.4 %all-to-all-start.9 = ((bf16[32,4,2560]{2,1,0:T(4,128)(2,1)}), bf16[32,4,2560]{2,1,0:T(4,128)(2,1)S(1)}, u32[]{:S(2)}, u32[]{:S(2)}) async-start(bf16[32,4,2560]{2,1,0:T(4,128)(2,1)} %gather_fusion.6), calls=%async_computation.9 | async-start | bytes 1310720 | tf_op jit(solution)/shard_map/all_to_all | solution.py:51
  270.7 15.4 %all-to-all-done.9 = bf16[32,4,2560]{2,1,0:T(4,128)(2,1)S(1)} async-done(((bf16[32,4,2560]{2,1,0:T(4,128)(2,1)}), bf16[32,4,2560]{2,1,0:T(4,128)(2,1)S(1)}, u32[]{:S(2)}, u32[]{:S(2)}) %all-to-all-start.9) | async-done | bytes 655392 | tf_op jit(solution)/shard_map/all_to_all | solution.py:51
  286.1 3.7 %all-to-all-start.11 = ((bf16[32,4,2560]{2,1,0:T(4,128)(2,1)}), bf16[32,4,2560]{2,1,0:T(4,128)(2,1)S(1)}, u32[]{:S(2)}, u32[]{:S(2)}) async-start(bf16[32,4,2560]{2,1,0:T(4,128)(2,1)} %gather_fusion.8), calls=%async_computation.11 | async-start | bytes 1310720 | tf_op jit(solution)/shard_map/all_to_all | solution.py:52
  291.8 2.2 gather_fusion.11
  297.1 10.5 %all-to-all-done.11 = bf16[32,4,2560]{2,1,0:T(4,128)(2,1)S(1)} async-done(((bf16[32,4,2560]{2,1,0:T(4,128)(2,1)}), bf16[32,4,2560]{2,1,0:T(4,128)(2,1)S(1)}, u32[]{:S(2)}, u32[]{:S(2)}) %all-to-all-start.11) | async-done | bytes 655392 | tf_op jit(solution)/shard_map/all_to_all | solution.py:52
  (141 shorter events, 83.7 us)
Async XLA Ops:
  4.9 5.3 %copy-start.8 = (s32[1024]{0:T(1024)S(1)}, s32[1024]{0:T(1024)}, u32[]{:S(2)}) copy-start(s32[1024]{0:T(1024)} %param.19) | copy-start | bytes 12292
  4.9 5.3 %copy-start.2 = (bf16[128,2560]{1,0:T(8,128)(2,1)S(1)}, bf16[128,2560]{1,0:T(8,128)(2,1)}, u32[]{:S(2)}) copy-start(bf16[128,2560]{1,0:T(8,128)(2,1)} %param.11) | copy-start | bytes 1966084
  6.0 14.5 %all-to-all-start.6 = ((bf16[128,4,5,128]{0,3,2,1:T(8,128)(2,1)}), bf16[128,4,5,128]{0,3,2,1:T(8,128)(2,1)S(1)}, u32[]{:S(2)}, u32[]{:S(2)}) async-start(bf16[128,4,5,128]{0,3,2,1:T(8,128)(2,1)} %fusion.32), calls=%async_computation.6 | async-start | bytes 1310720 | tf_op jit(solution)/shard_map/all_to_all | solution.py:116
  10.5 15.5 %copy-start.3 = (bf16[128,2560]{1,0:T(8,128)(2,1)S(1)}, bf16[128,2560]{1,0:T(8,128)(2,1)}, u32[]{:S(2)}) copy-start(bf16[128,2560]{1,0:T(8,128)(2,1)} %param.12) | copy-start | bytes 1966084
  20.4 23.5 %all-to-all-start = ((bf16[32,4,2560]{2,1,0:T(4,128)(2,1)}), bf16[32,4,2560]{2,1,0:T(4,128)(2,1)S(1)}, u32[]{:S(2)}, u32[]{:S(2)}) async-start(bf16[32,4,2560]{2,1,0:T(4,128)(2,1)} %gather_fusion), calls=%async_computation | async-start | bytes 1310720 | tf_op jit(solution)/shard_map/all_to_all | solution.py:43
  26.2 21.3 %copy-start.4 = (bf16[128,2560]{1,0:T(8,128)(2,1)S(1)}, bf16[128,2560]{1,0:T(8,128)(2,1)}, u32[]{:S(2)}) copy-start(bf16[128,2560]{1,0:T(8,128)(2,1)} %param.13) | copy-start | bytes 1966084
  44.0 21.4 %all-to-all-start.2 = ((bf16[32,4,2560]{2,1,0:T(4,128)(2,1)}), bf16[32,4,2560]{2,1,0:T(4,128)(2,1)S(1)}, u32[]{:S(2)}, u32[]{:S(2)}) async-start(bf16[32,4,2560]{2,1,0:T(4,128)(2,1)} %gather_fusion.2), calls=%async_computation.2 | async-start | bytes 1310720 | tf_op jit(solution)/shard_map/all_to_all | solution.py:44
  65.4 21.4 %all-to-all-start.4 = ((bf16[32,4,2560]{2,1,0:T(4,128)(2,1)}), bf16[32,4,2560]{2,1,0:T(4,128)(2,1)S(1)}, u32[]{:S(2)}, u32[]{:S(2)}) async-start(bf16[32,4,2560]{2,1,0:T(4,128)(2,1)} %gather_fusion.4), calls=%async_computation.4 | async-start | bytes 1310720 | tf_op jit(solution)/shard_map/all_to_all | solution.py:45
  86.8 14.5 %all-to-all-start.1 = ((bf16[128,4,5,128]{3,0,2,1:T(8,128)(2,1)}), bf16[128,4,5,128]{3,0,2,1:T(8,128)(2,1)}, u32[]{:S(2)}, u32[]{:S(2)}) async-start(bf16[128,4,5,128]{3,0,2,1:T(8,128)(2,1)} %copy.72), calls=%async_computation.1 | async-start | bytes 1310720 | tf_op jit(solution)/shard_map/all_to_all | solution.py:109
  101.3 13.7 %all-to-all-start.3 = ((bf16[128,4,5,128]{3,0,2,1:T(8,128)(2,1)}), bf16[128,4,5,128]{3,0,2,1:T(8,128)(2,1)S(1)}, u32[]{:S(2)}, u32[]{:S(2)}) async-start(bf16[128,4,5,128]{3,0,2,1:T(8,128)(2,1)} %copy.74), calls=%async_computation.3 | async-start | bytes 1310720 | tf_op jit(solution)/shard_map/all_to_all | solution.py:112
  115.0 13.7 %all-to-all-start.5 = ((bf16[128,4,5,128]{3,0,2,1:T(8,128)(2,1)}), bf16[128,4,5,128]{3,0,2,1:T(8,128)(2,1)S(1)}, u32[]{:S(2)}, u32[]{:S(2)}) async-start(bf16[128,4,5,128]{3,0,2,1:T(8,128)(2,1)} %copy.76), calls=%async_computation.5 | async-start | bytes 1310720 | tf_op jit(solution)/shard_map/all_to_all | solution.py:113
  170.6 3.7 %copy-start.5 = (bf16[5,512,128]{2,1,0:T(8,128)(2,1)S(1)}, bf16[5,512,128]{2,1,0:T(8,128)(2,1)}, u32[]{:S(2)}) copy-start(bf16[5,512,128]{2,1,0:T(8,128)(2,1)} %get-tuple-element.62) | copy-start | bytes 1966084
  170.6 18.1 %all-to-all-start.7 = ((bf16[512,1,5,128]{3,2,1,0:T(8,128)(2,1)}), bf16[512,1,5,128]{3,2,1,0:T(8,128)(2,1)S(1)}, u32[]{:S(2)}, u32[]{:S(2)}) async-start(bf16[512,1,5,128]{3,2,1,0:T(8,128)(2,1)} %copy.85), calls=%async_computation.7 | async-start | bytes 2097152 | tf_op jit(solution)/shard_map/all_to_all | solution.py:129
  175.8 17.5 %copy-start.7 = (bf16[5,512,128]{2,1,0:T(8,128)(2,1)S(1)}, bf16[5,512,128]{2,1,0:T(8,128)(2,1)}, u32[]{:S(2)}) copy-start(bf16[5,512,128]{2,1,0:T(8,128)(2,1)} %get-tuple-element.60) | copy-start | bytes 1966084
  188.7 1.0 copy-start
  189.7 18.0 %all-to-all-start.12 = ((bf16[512,1,5,128]{3,2,1,0:T(8,128)(2,1)}), bf16[512,1,5,128]{3,2,1,0:T(8,128)(2,1)S(1)}, u32[]{:S(2)}, u32[]{:S(2)}) async-start(bf16[512,1,5,128]{3,2,1,0:T(8,128)(2,1)} %copy.93), calls=%async_computation.12 | async-start | bytes 2097152 | tf_op jit(solution)/shard_map/all_to_all | solution.py:132
  194.7 16.5 %copy-start.6 = (bf16[5,512,128]{2,1,0:T(8,128)(2,1)S(1)}, bf16[5,512,128]{2,1,0:T(8,128)(2,1)}, u32[]{:S(2)}) copy-start(bf16[5,512,128]{2,1,0:T(8,128)(2,1)} %get-tuple-element.61) | copy-start | bytes 1966084
  207.7 18.0 %all-to-all-start.8 = ((bf16[512,1,5,128]{3,2,1,0:T(8,128)(2,1)}), bf16[512,1,5,128]{3,2,1,0:T(8,128)(2,1)S(1)}, u32[]{:S(2)}, u32[]{:S(2)}) async-start(bf16[512,1,5,128]{3,2,1,0:T(8,128)(2,1)} %copy.89), calls=%async_computation.8 | async-start | bytes 2097152 | tf_op jit(solution)/shard_map/all_to_all | solution.py:130
  225.6 18.0 %all-to-all-start.10 = ((bf16[512,1,5,128]{3,2,1,0:T(8,128)(2,1)}), bf16[512,1,5,128]{3,2,1,0:T(8,128)(2,1)S(1)}, u32[]{:S(2)}, u32[]{:S(2)}) async-start(bf16[512,1,5,128]{3,2,1,0:T(8,128)(2,1)} %copy.91), calls=%async_computation.10 | async-start | bytes 2097152 | tf_op jit(solution)/shard_map/all_to_all | solution.py:131
  243.6 21.2 %all-to-all-start.13 = ((bf16[32,4,2560]{2,1,0:T(4,128)(2,1)}), bf16[32,4,2560]{2,1,0:T(4,128)(2,1)}, u32[]{:S(2)}, u32[]{:S(2)}) async-start(bf16[32,4,2560]{2,1,0:T(4,128)(2,1)} %gather_fusion.10), calls=%async_computation.13 | async-start | bytes 1310720 | tf_op jit(solution)/shard_map/all_to_all | solution.py:53
  264.8 21.3 %all-to-all-start.9 = ((bf16[32,4,2560]{2,1,0:T(4,128)(2,1)}), bf16[32,4,2560]{2,1,0:T(4,128)(2,1)S(1)}, u32[]{:S(2)}, u32[]{:S(2)}) async-start(bf16[32,4,2560]{2,1,0:T(4,128)(2,1)} %gather_fusion.6), calls=%async_computation.9 | async-start | bytes 1310720 | tf_op jit(solution)/shard_map/all_to_all | solution.py:51
  268.8 21.2 %copy-start.1 = (bf16[512,1,5,128]{3,2,1,0:T(8,128)(2,1)S(1)}, bf16[512,1,5,128]{3,2,1,0:T(8,128)(2,1)}, u32[]{:S(2)}) copy-start(bf16[512,1,5,128]{3,2,1,0:T(8,128)(2,1)} %copy-done) | copy-start | bytes 1966084
  286.1 21.4 %all-to-all-start.11 = ((bf16[32,4,2560]{2,1,0:T(4,128)(2,1)}), bf16[32,4,2560]{2,1,0:T(4,128)(2,1)S(1)}, u32[]{:S(2)}, u32[]{:S(2)}) async-start(bf16[32,4,2560]{2,1,0:T(4,128)(2,1)} %gather_fusion.8), calls=%async_computation.11 | async-start | bytes 1310720 | tf_op jit(solution)/shard_map/all_to_all | solution.py:52
where the time goes:
time: 311 us; the launch traced here: 310 us
  waiting for transfers between devices  165 us (53%)
  starting transfers between devices  52.8 us (17%)
  local copies, waits for them, and re-layouts  52.3 us (17%)
  matrix products  29.8 us (10%)
  other arithmetic  8.28 us (3%)
    all_to_all x1, waiting for transfers between devices, dispatch(): lax.all_to_all(second, ('dp', 'sp'), split_axis=0, concat_axis=0, tiled=T...  15.8 us
    all_to_all x1, waiting for transfers between devices, dispatch(): lax.all_to_all(first, ('dp', 'sp'), split_axis=0, concat_axis=0, tiled=True)  15.8 us
    all_to_all x1, waiting for transfers between devices, send_back(): lax.all_to_all(third, ('dp', 'sp'), split_axis=0, concat_axis=0, tiled=True)  15.4 us
    all_to_all x1, waiting for transfers between devices, send_back(): lax.all_to_all(first, ('dp', 'sp'), split_axis=0, concat_axis=0, tiled=True)  15.4 us
    all_to_all x1, waiting for transfers between devices, per_device(): lax.all_to_all(gv_heads, 'sp', split_axis=0, concat_axis=1, tiled=True)  13 us
    all_to_all x1, waiting for transfers between devices, per_device(): lax.all_to_all(gq_heads, 'sp', split_axis=0, concat_axis=1, tiled=True)  12.9 us
    all_to_all x1, waiting for transfers between devices, per_device(): lax.all_to_all(out_heads, 'sp', split_axis=0, concat_axis=1, tiled=True)  12.9 us
    all_to_all x1, waiting for transfers between devices, dispatch(): lax.all_to_all(third, ('dp', 'sp'), split_axis=0, concat_axis=0, tiled=True)  12.9 us
  transfers between devices with their start and end apart: 14, of which 14 were waited for; matrix products, arithmetic and copies ran while one was open for 13% of the time, Pallas kernels for 0%

commit v1 on v0

--- a/solution.py
+++ b/solution.py
@@ -1,10 +1,17 @@
+import functools
+
 import jax
 import jax.numpy as jnp
 from jax import lax
+from jax.experimental import pallas as pl
+from jax.experimental.pallas import tpu as pltpu
 from jax.sharding import PartitionSpec as P
 
 HEADS = 20
 HD = 128
+MESH = pl.DeviceIdType.MESH
+F32 = jnp.float32
+BF16 = jnp.bfloat16
 
 
 def head_pass(query_head, key_head, value_head, grad_head, query_live, key_live):
@@ -150,6 +157,370 @@
     return (attn_out, grad_queries, grad_keys, grad_values)
 
 
+def dot_nn(left, right):
+    return lax.dot_general(left, right, (((1,), (0,)), ((), ())), preferred_element_type=F32)
+
+
+def dot_nt(left, right):
+    return lax.dot_general(left, right, (((1,), (1,)), ((), ())), preferred_element_type=F32)
+
+
+def dot_tn(left, right):
+    return lax.dot_general(left, right, (((0,), (0,)), ((), ())), preferred_element_type=F32)
+
+
+def iota(shape, axis):
+    return lax.broadcasted_iota(jnp.int32, shape, axis)
+
+
+def fused_kernel(
+    n_dp,
+    n_sp,
+    block_rows,
+    heads_dev,
+    length_ref,
+    plan_ref,
+    bin_ref,
+    table_ref,
+    source_ref,
+    q_ref,
+    k_ref,
+    v_ref,
+    cot_ref,
+    out_ref,
+    gq_ref,
+    gk_ref,
+    gv_ref,
+    send_buf,
+    recv_buf,
+    cot_buf,
+    grad_buf,
+    back_buf,
+    out_buf,
+    oback_buf,
+    order_buf,
+    unorder_buf,
+    pick_buf,
+    send_sem,
+    recv_sem,
+    gsend_sem,
+    back_sem,
+    csend_sem,
+    crecv_sem,
+    osend_sem,
+    orecv_sem,
+    local_sem,
+):
+    n = n_dp * n_sp
+    chunk = n_sp * block_rows
+    tok = q_ref.shape[0]
+    group_tok = tok * n_sp
+    group_blocks = group_tok // block_rows
+    others = (n - 1) * chunk
+    group = lax.axis_index("dp")
+    part = lax.axis_index("sp")
+    me = group * n_sp + part
+    my_rows = pl.ds(pl.multiple_of(me * chunk, chunk), chunk)
+    my_group_rows = pl.ds(pl.multiple_of(group * chunk, chunk), chunk)
+    my_part_rows = pl.ds(pl.multiple_of(part * tok, tok), tok)
+
+    barrier = pltpu.get_barrier_semaphore()
+
+    def greet(i, carry):
+        peer = (me + 1 + i) % n
+        pl.semaphore_signal(
+            barrier, inc=1, device_id=(peer // n_sp, peer % n_sp), device_id_type=MESH
+        )
+        return carry
+
+    lax.fori_loop(0, n - 1, greet, 0)
+
+    source = source_ref[...]
+    loader_of = source // n
+    mine = jnp.where(loader_of == me, source % n, 0)
+    spread = jnp.broadcast_to(mine[:, None, :], (n_dp, chunk, group_blocks)).reshape(
+        n_dp * chunk, group_blocks
+    )
+    row_part = (iota((n_dp * chunk, group_blocks), 0) // block_rows) % n_sp
+    col_part = iota((n_dp * chunk, group_blocks), 1) // n
+    slot = jnp.sum(jnp.where(row_part == col_part, spread, 0), axis=1, keepdims=True)
+    pick_row = slot * block_rows + iota((n_dp * chunk, 1), 0) % block_rows
+    pick_buf[...] = jnp.where(iota((n_dp * chunk, tok), 1) == pick_row, 1.0, 0.0).astype(BF16)
+
+    def prepare(j):
+        for part_to in range(n_sp):
+            head = part_to * heads_dev + j
+            columns = pl.ds(pl.multiple_of(head * HD, HD), HD)
+            for which, ref in enumerate((q_ref, k_ref, v_ref)):
+                send_buf[head, which] = dot_nn(pick_buf[...], ref[:, columns]).astype(BF16)
+
+    def peer_at(i):
+        turn = n // 2 + i
+        peer = (me + turn % n + turn // n) % n
+        return peer // n_sp, peer % n_sp
+
+    def forward(j):
+        def one(i, carry):
+            to_group, to_part = peer_at(i)
+            pltpu.make_async_remote_copy(
+                src_ref=send_buf.at[
+                    to_part * heads_dev + j,
+                    :,
+                    pl.ds(pl.multiple_of(to_group * chunk, chunk), chunk),
+                    :,
+                ],
+                dst_ref=recv_buf.at[j, :, my_rows, :],
+                send_sem=send_sem.at[j],
+                recv_sem=recv_sem.at[j],
+                device_id=(to_group, to_part),
+                device_id_type=MESH,
+            ).start()
+            return carry
+
+        lax.fori_loop(0, n - 1, one, 0)
+        pltpu.make_async_copy(
+            send_buf.at[part * heads_dev + j, :, my_group_rows, :],
+            recv_buf.at[j, :, my_rows, :],
+            local_sem.at[j],
+        ).start()
+
+    def backward(j):
+        def one(i, carry):
+            to_group, to_part = peer_at(i)
+            to = to_group * n_sp + to_part
+            pltpu.make_async_remote_copy(
+                src_ref=grad_buf.at[j, :, pl.ds(pl.multiple_of(to * chunk, chunk), chunk), :],
+                dst_ref=back_buf.at[part * heads_dev + j, :, my_group_rows, :],
+                send_sem=gsend_sem.at[j],
+                recv_sem=back_sem.at[j],
+                device_id=(to_group, to_part),
+                device_id_type=MESH,
+            ).start()
+            return carry
+
+        lax.fori_loop(0, n - 1, one, 0)
+        pltpu.make_async_copy(
+            grad_buf.at[j, :, my_rows, :],
+            back_buf.at[part * heads_dev + j, :, my_group_rows, :],
+            local_sem.at[heads_dev + j],
+        ).start()
+
+        for step in range(1, n_sp):
+            to_part = (part + step) % n_sp
+            pltpu.make_async_remote_copy(
+                src_ref=out_buf.at[j, pl.ds(pl.multiple_of(to_part * tok, tok), tok), :],
+                dst_ref=oback_buf.at[part * heads_dev + j],
+                send_sem=osend_sem.at[j],
+                recv_sem=orecv_sem.at[j],
+                device_id=(group, to_part),
+                device_id_type=MESH,
+            ).start()
+        pltpu.make_async_copy(
+            out_buf.at[j, my_part_rows, :],
+            oback_buf.at[part * heads_dev + j],
+            local_sem.at[2 * heads_dev + j],
+        ).start()
+
+    def wait_bytes(ref, sem):
+        pltpu.make_async_copy(ref, ref, sem).wait()
+
+    width = heads_dev * HD
+    prepare(0)
+    pl.semaphore_wait(barrier, n - 1)
+    forward(0)
+    for step in range(1, n_sp):
+        to_part = (part + step) % n_sp
+        pltpu.make_async_remote_copy(
+            src_ref=cot_ref.at[:, pl.ds(pl.multiple_of(to_part * width, HD), width)],
+            dst_ref=cot_buf.at[my_part_rows, :],
+            send_sem=csend_sem,
+            recv_sem=crecv_sem,
+            device_id=(group, to_part),
+            device_id_type=MESH,
+        ).start()
+    pltpu.make_async_copy(
+        cot_ref.at[:, pl.ds(pl.multiple_of(part * width, HD), width)],
+        cot_buf.at[my_part_rows, :],
+        local_sem.at[3 * heads_dev],
+    ).start()
+
+    def send_more(j, carry):
+        prepare(j)
+        forward(j)
+        return carry
+
+    lax.fori_loop(1, heads_dev, send_more, 0)
+
+    group_len = jnp.int32(0)
+    group_bin = jnp.int32(0)
+    for sample in range(n_dp):
+        picked = plan_ref[sample] == group
+        group_len += jnp.where(picked, length_ref[sample], 0)
+        group_bin += jnp.where(picked, bin_ref[sample], 0)
+
+    loader_row = (source_ref[pl.ds(group, 1), :] // n).astype(F32)
+    widen = jnp.where(
+        iota((group_blocks, group_tok), 0) == iota((group_blocks, group_tok), 1) // block_rows,
+        1.0,
+        0.0,
+    ).astype(BF16)
+    place = iota((1, group_tok), 1)
+    lane_loader = dot_nn(
+        jnp.broadcast_to(loader_row, (16, group_blocks)).astype(BF16), widen
+    )[0:1].astype(jnp.int32)
+    lane_row = lane_loader * chunk + (place // tok) * block_rows + place % block_rows
+    col_loader = jnp.sum(
+        jnp.where(
+            iota((group_tok, group_blocks), 1) == iota((group_tok, group_blocks), 0) // block_rows,
+            loader_row,
+            0.0,
+        ),
+        axis=1,
+        keepdims=True,
+    ).astype(jnp.int32)
+    col_place = iota((group_tok, 1), 0)
+    col_row = col_loader * chunk + (col_place // tok) * block_rows + col_place % block_rows
+    square = (group_tok, group_tok)
+    order = jnp.where(iota(square, 0) == lane_row, 1.0, 0.0)
+    unorder = jnp.where(iota(square, 1) == col_row, 1.0, 0.0)
+    order_buf[...] = order.astype(BF16)
+    unorder_buf[...] = unorder.astype(BF16)
+    key_live = jnp.sum(jnp.where(place < group_len, order, 0.0), axis=1, keepdims=True)
+    query_live = jnp.sum(jnp.where(col_place < group_len, unorder, 0.0), axis=0, keepdims=True)
+
+    wait_bytes(cot_buf.at[pl.ds(0, (n_sp - 1) * tok), :], crecv_sem)
+    wait_bytes(cot_buf.at[my_part_rows, :], local_sem.at[3 * heads_dev])
+
+    scale = HD ** (-0.5)
+
+    def one_head(j, carry):
+        gate = table_ref[group_bin, part * heads_dev + j]
+        columns = pl.ds(pl.multiple_of(j * HD, HD), HD)
+        d_out = (gate * dot_nn(order_buf[...], cot_buf[:, columns])).astype(BF16)
+        wait_bytes(recv_buf.at[j, :, pl.ds(0, others), :], recv_sem.at[j])
+        wait_bytes(recv_buf.at[j, :, my_rows, :], local_sem.at[j])
+        query, key, value = recv_buf[j, 0], recv_buf[j, 1], recv_buf[j, 2]
+        scores = dot_nt(key, query) * scale
+        scores = jnp.where(key_live > 0.5, scores, -1e30)
+        top = jnp.max(scores, axis=0, keepdims=True)
+        shifted = jnp.exp(scores - top)
+        total = jnp.sum(shifted, axis=0, keepdims=True)
+        attend = shifted * (query_live / total)
+        attend_bf = attend.astype(BF16)
+        grad_attend = dot_nt(value, d_out)
+        row_dot = jnp.sum(attend_bf.astype(F32) * grad_attend, axis=0, keepdims=True)
+        grad_scores = (attend * (grad_attend - row_dot) * scale).astype(BF16)
+        grad_buf[j, 2] = dot_nn(attend_bf, d_out).astype(BF16)
+        grad_buf[j, 1] = dot_nn(grad_scores, query).astype(BF16)
+        grad_buf[j, 0] = dot_tn(grad_scores, key).astype(BF16)
+        output = dot_tn(attend_bf, value).astype(BF16)
+        gated = (gate * output.astype(F32)).astype(BF16)
+        out_buf[j] = dot_nn(unorder_buf[...], gated).astype(BF16)
+        backward(j)
+        return carry
+
+    lax.fori_loop(0, heads_dev, one_head, 0)
+
+    def collect(j, carry):
+        wait_bytes(recv_buf.at[j, :, pl.ds(0, others), :], back_sem.at[j])
+        wait_bytes(recv_buf.at[j, :, my_rows, :], local_sem.at[heads_dev + j])
+        wait_bytes(out_buf.at[j, pl.ds(0, (n_sp - 1) * tok), :], orecv_sem.at[j])
+        wait_bytes(out_buf.at[j, my_part_rows, :], local_sem.at[2 * heads_dev + j])
+        for part_from in range(n_sp):
+            head = part_from * heads_dev + j
+            columns = pl.ds(pl.multiple_of(head * HD, HD), HD)
+            out_ref[:, columns] = oback_buf[head]
+            for which, ref in enumerate((gq_ref, gk_ref, gv_ref)):
+                ref[:, columns] = dot_tn(pick_buf[...], back_buf[head, which]).astype(BF16)
+        return carry
+
+    lax.fori_loop(0, heads_dev, collect, 0)
+
+    def drain(j, carry):
+        wait_bytes(recv_buf.at[j, :, pl.ds(0, others), :], send_sem.at[j])
+        wait_bytes(recv_buf.at[j, :, pl.ds(0, others), :], gsend_sem.at[j])
+        wait_bytes(out_buf.at[j, pl.ds(0, (n_sp - 1) * tok), :], osend_sem.at[j])
+        return carry
+
+    lax.fori_loop(0, heads_dev, drain, 0)
+    wait_bytes(cot_buf.at[pl.ds(0, (n_sp - 1) * tok), :], csend_sem)
+
+
+def fused(
+    n_dp,
+    n_sp,
+    queries,
+    key_rows,
+    value_rows,
+    cotangent,
+    lengths,
+    sample_plan,
+    guide_bins,
+    guide_table,
+    block_source,
+):
+    tok, row_width = queries.shape
+    n = n_dp * n_sp
+    heads_dev = HEADS // n_sp
+    group_tok = tok * n_sp
+    smem = pl.BlockSpec(memory_space=pltpu.SMEM)
+    vmem = pl.BlockSpec(memory_space=pltpu.VMEM)
+    flops = 2 * 8 * heads_dev * group_tok * group_tok * HD
+    return pl.pallas_call(
+        functools.partial(fused_kernel, n_dp, n_sp, tok // n, heads_dev),
+        out_shape=[jax.ShapeDtypeStruct((tok, row_width), BF16)] * 4,
+        in_specs=[smem] * 4 + [vmem] * 5,
+        out_specs=[vmem] * 4,
+        scratch_shapes=[
+            pltpu.VMEM((HEADS, 3, tok, HD), BF16),
+            pltpu.VMEM((heads_dev, 3, group_tok, HD), BF16),
+            pltpu.VMEM((group_tok, heads_dev * HD), BF16),
+            pltpu.VMEM((heads_dev, 3, group_tok, HD), BF16),
+            pltpu.VMEM((HEADS, 3, tok, HD), BF16),
+            pltpu.VMEM((heads_dev, group_tok, HD), BF16),
+            pltpu.VMEM((HEADS, tok, HD), BF16),
+            pltpu.VMEM((group_tok, group_tok), BF16),
+            pltpu.VMEM((group_tok, group_tok), BF16),
+            pltpu.VMEM((tok, tok), BF16),
+            pltpu.SemaphoreType.DMA((heads_dev,)),
+            pltpu.SemaphoreType.DMA((heads_dev,)),
+            pltpu.SemaphoreType.DMA((heads_dev,)),
+            pltpu.SemaphoreType.DMA((heads_dev,)),
+            pltpu.SemaphoreType.DMA,
+            pltpu.SemaphoreType.DMA,
+            pltpu.SemaphoreType.DMA((heads_dev,)),
+            pltpu.SemaphoreType.DMA((heads_dev,)),
+            pltpu.SemaphoreType.DMA((3 * heads_dev + 1,)),
+        ],
+        compiler_params=pltpu.CompilerParams(
+            collective_id=0, has_side_effects=True, vmem_limit_bytes=48 * 1024 * 1024
+        ),
+        cost_estimate=pl.CostEstimate(
+            flops=flops, bytes_accessed=16 * tok * row_width, transcendentals=0
+        ),
+        name="routed_attention",
+    )(
+        lengths,
+        sample_plan,
+        guide_bins,
+        guide_table,
+        block_source.reshape(n_dp, block_source.shape[0] // n_dp),
+        queries,
+        key_rows,
+        value_rows,
+        cotangent,
+    )
+
+
+def chosen(*arrays):
+    n_dp, n_sp = lax.axis_size("dp"), lax.axis_size("sp")
+    tok = arrays[0].shape[0]
+    block_rows = tok // (n_dp * n_sp)
+    if (n_sp * block_rows) % 16 == 0 and HEADS % n_sp == 0:
+        return fused(n_dp, n_sp, *arrays)
+    return per_device(*arrays)
+
+
 def solution(mesh):
     placed = (
         P(("dp", "sp"), None),
@@ -163,7 +534,7 @@
         P(),
     )
     return jax.shard_map(
-        per_device,
+        chosen,
         mesh=mesh,
         in_specs=placed,
         out_specs=(

time: 311 us -> 105 us (0.34)
  waiting for transfers between devices: 165 us -> 0 us
  Pallas kernels: 0 us -> 94.5 us
  starting transfers between devices: 52.8 us -> 0 us
  local copies, waits for them, and re-layouts: 52.3 us -> 9.73 us
  matrix products: 29.8 us -> 0 us
  other arithmetic: 8.28 us -> 0 us
    all_to_all x14 -> x0, waiting for transfers between devices: 165 us -> none  [the longest x1 15.8 us: dispatch(): lax.all_to_all(second, ('dp', 'sp'), split_axis=0, concat_axis=0, tiled=T...]
    pallas_call x0 -> x1, Pallas kernels: none -> 94.5 us  [fused(): pl.pallas_call(functools.partial(fused_kernel, n_dp, n_sp, tok // n, head...]
    all_to_all x14 -> x0, starting transfers between devices: 52.8 us -> none  [the longest x1 5.62 us: dispatch(): lax.all_to_all(first, ('dp', 'sp'), split_axis=0, concat_axis=0, tiled=True)]
    dot_general x30 -> x0, matrix products: 29.8 us -> none  [the longest x5 6.78 us: head_pass(): jnp.dot(grad_head, value_head.T, preferred_element_type=jnp.float32)]
    gather x12 -> x0, local copies, waits for them, and re-layouts: 19.9 us -> none  [the longest x6 11.4 us: as_blocks(): return source.reshape(loaders, block_rows, row_width)[order]]
    another operation x9 -> x0, local copies, waits for them, and re-layouts: 9.37 us -> none  [the longest x2 3.06 us: per_device(): query_own.reshape(split_shape)]
    convert_element_type x5 -> x0, local copies, waits for them, and re-layouts: 7.26 us -> none  [the longest x4 6.93 us: per_device(): jnp.moveaxis(result, 0, 1)[:, None].astype(jnp.bfloat16)]
    unnamed x20 -> x22, local copies, waits for them, and re-layouts: 3.52 us -> 9.73 us
  transfers between devices with their start and end apart: 14 -> 0, of which waited for: 14 -> 0; matrix products, arithmetic and copies ran while one was open for 13% -> 0% of each run, Pallas kernels for 0% -> 0%
where the time goes in v1:
time: 105 us
  Pallas kernels  94.5 us (90%)
  local copies, waits for them, and re-layouts  9.73 us (9%)
    pallas_call x1, Pallas kernels, fused(): pl.pallas_call(functools.partial(fused_kernel, n_dp, n_sp, tok // n, head...  94.5 us
    unnamed x22, local copies, waits for them, and re-layouts  9.73 us

profile of v1, /device:TPU:0, one launch (start us, length us, event | category | flops | bytes accessed | tf_op | source)
XLA Modules:
  0.0 104.9 jit_solution(13280476576794853236)
XLA Ops:
  0.6 0.0 copy-start.8
  0.6 0.0 copy-start.7
  0.7 0.0 copy-start.6
  0.7 0.6 copy-done.8
  1.3 0.0 copy-done.7
  1.3 0.0 copy-done.6
  1.3 0.0 copy-start
  1.3 1.1 %copy-done = bf16[128,2560]{1,0:T(8,128)(2,1)S(1)} copy-done((bf16[128,2560]{1,0:T(8,128)(2,1)S(1)}, bf16[128,2560]{1,0:T(8,128)(2,1)}, u32[]{:S(2)}) %copy-start) | copy-done | bytes 655384
  2.4 0.0 copy-start.1
  2.4 1.1 %copy-done.1 = bf16[128,2560]{1,0:T(8,128)(2,1)S(1)} copy-done((bf16[128,2560]{1,0:T(8,128)(2,1)S(1)}, bf16[128,2560]{1,0:T(8,128)(2,1)}, u32[]{:S(2)}) %copy-start.1) | copy-done | bytes 655384
  3.5 0.0 copy-start.2
  3.5 1.1 %copy-done.2 = bf16[128,2560]{1,0:T(8,128)(2,1)S(1)} copy-done((bf16[128,2560]{1,0:T(8,128)(2,1)S(1)}, bf16[128,2560]{1,0:T(8,128)(2,1)}, u32[]{:S(2)}) %copy-start.2) | copy-done | bytes 655384
  4.6 0.0 copy-start.3
  4.6 1.1 %copy-done.3 = bf16[128,2560]{1,0:T(8,128)(2,1)S(1)} copy-done((bf16[128,2560]{1,0:T(8,128)(2,1)S(1)}, bf16[128,2560]{1,0:T(8,128)(2,1)}, u32[]{:S(2)}) %copy-start.3) | copy-done | bytes 655384
  5.7 0.0 copy-start.4
  5.7 0.7 copy-done.4
  6.4 0.0 copy-start.5
  6.4 0.7 copy-done.5
  7.0 94.5 %routed_attention.1 = (bf16[128,2560]{1,0:T(8,128)(2,1)S(1)}, bf16[128,2560]{1,0:T(8,128)(2,1)S(1)}, bf16[128,2560]{1,0:T(8,128)(2,1)S(1)}, bf16[128,2560]{1,0:T(8,128)(2,1)S(1)}) custom-call(s32[8]{0:T(128)S(1)} %copy-done.6, s32[8]{0:T(128)S(1)} %copy-done.7, s32[8]{0:T(128)S(1)} %copy-done.8, f32[8,20]{1,0:T(8,128)S(1)} %copy-done.4, ...), custom_call_target="tpu_custom_call" | custom-call | flops 2684354560 | bytes 5242880 | tf_op jit(solution)/shard_map/routed_attention/pallas_call | solution.py:469
  101.5 0.8 copy.17
  102.4 0.8 copy.18
  103.2 0.8 copy.19
  104.1 0.8 copy.20
Async XLA Ops:
  0.6 0.7 copy-start.8
  0.6 0.7 copy-start.7
  0.7 0.7 copy-start.6
  1.3 1.1 %copy-start = (bf16[128,2560]{1,0:T(8,128)(2,1)S(1)}, bf16[128,2560]{1,0:T(8,128)(2,1)}, u32[]{:S(2)}) copy-start(bf16[128,2560]{1,0:T(8,128)(2,1)} %q_ref.1) | copy-start | bytes 1966084
  2.4 1.1 %copy-start.1 = (bf16[128,2560]{1,0:T(8,128)(2,1)S(1)}, bf16[128,2560]{1,0:T(8,128)(2,1)}, u32[]{:S(2)}) copy-start(bf16[128,2560]{1,0:T(8,128)(2,1)} %k_ref.1) | copy-start | bytes 1966084
  3.5 1.1 %copy-start.2 = (bf16[128,2560]{1,0:T(8,128)(2,1)S(1)}, bf16[128,2560]{1,0:T(8,128)(2,1)}, u32[]{:S(2)}) copy-start(bf16[128,2560]{1,0:T(8,128)(2,1)} %v_ref.1) | copy-start | bytes 1966084
  4.6 1.1 %copy-start.3 = (bf16[128,2560]{1,0:T(8,128)(2,1)S(1)}, bf16[128,2560]{1,0:T(8,128)(2,1)}, u32[]{:S(2)}) copy-start(bf16[128,2560]{1,0:T(8,128)(2,1)} %cot_ref.1) | copy-start | bytes 1966084
  5.7 0.7 copy-start.4
  6.4 0.7 copy-start.5

commit v2 on v1

--- a/solution.py
+++ b/solution.py
@@ -10,6 +10,7 @@
 HEADS = 20
 HD = 128
 MESH = pl.DeviceIdType.MESH
+VMEM_GRANT = 62 * 1024 * 1024
 F32 = jnp.float32
 BF16 = jnp.bfloat16
 
@@ -191,6 +192,7 @@
     gq_ref,
     gk_ref,
     gv_ref,
+    load_buf,
     send_buf,
     recv_buf,
     cot_buf,
@@ -201,6 +203,8 @@
     order_buf,
     unorder_buf,
     pick_buf,
+    stage_buf,
+    load_sem,
     send_sem,
     recv_sem,
     gsend_sem,
@@ -210,6 +214,7 @@
     osend_sem,
     orecv_sem,
     local_sem,
+    store_sem,
 ):
     n = n_dp * n_sp
     chunk = n_sp * block_rows
@@ -224,7 +229,17 @@
     my_group_rows = pl.ds(pl.multiple_of(group * chunk, chunk), chunk)
     my_part_rows = pl.ds(pl.multiple_of(part * tok, tok), tok)
 
+    def load(j, carry):
+        for part_to in range(n_sp):
+            columns = pl.ds(pl.multiple_of((part_to * heads_dev + j) * HD, HD), HD)
+            for which, ref in enumerate((q_ref, k_ref, v_ref)):
+                pltpu.make_async_copy(
+                    ref.at[:, columns], load_buf.at[j, part_to, which], load_sem.at[j]
+                ).start()
+        return carry
+
     barrier = pltpu.get_barrier_semaphore()
+    load(0, 0)
 
     def greet(i, carry):
         peer = (me + 1 + i) % n
@@ -234,6 +249,7 @@
         return carry
 
     lax.fori_loop(0, n - 1, greet, 0)
+    lax.fori_loop(1, heads_dev, load, 0)
 
     source = source_ref[...]
     loader_of = source // n
@@ -247,16 +263,23 @@
     pick_row = slot * block_rows + iota((n_dp * chunk, 1), 0) % block_rows
     pick_buf[...] = jnp.where(iota((n_dp * chunk, tok), 1) == pick_row, 1.0, 0.0).astype(BF16)
 
+    def wait_bytes(ref, sem):
+        pltpu.make_async_copy(ref, ref, sem).wait()
+
     def prepare(j):
+        wait_bytes(load_buf.at[j], load_sem.at[j])
         for part_to in range(n_sp):
             head = part_to * heads_dev + j
-            columns = pl.ds(pl.multiple_of(head * HD, HD), HD)
-            for which, ref in enumerate((q_ref, k_ref, v_ref)):
-                send_buf[head, which] = dot_nn(pick_buf[...], ref[:, columns]).astype(BF16)
+            for which in range(3):
+                send_buf[head, which] = dot_nn(
+                    pick_buf[...], load_buf[j, part_to, which]
+                ).astype(BF16)
 
     def peer_at(i):
-        turn = n // 2 + i
-        peer = (me + turn % n + turn // n) % n
+        turn = i + (i + n - 3) // (n - 1)
+        quarter = n // 4
+        outer = (me // quarter + 6 - turn % 4) % 4
+        peer = outer * quarter + (me % quarter + turn // 4) % quarter
         return peer // n_sp, peer % n_sp
 
     def forward(j):
@@ -320,9 +343,6 @@
             oback_buf.at[part * heads_dev + j],
             local_sem.at[2 * heads_dev + j],
         ).start()
-
-    def wait_bytes(ref, sem):
-        pltpu.make_async_copy(ref, ref, sem).wait()
 
     width = heads_dev * HD
     prepare(0)
@@ -429,9 +449,14 @@
         for part_from in range(n_sp):
             head = part_from * heads_dev + j
             columns = pl.ds(pl.multiple_of(head * HD, HD), HD)
-            out_ref[:, columns] = oback_buf[head]
+            pltpu.make_async_copy(
+                oback_buf.at[head], out_ref.at[:, columns], store_sem.at[0]
+            ).start()
             for which, ref in enumerate((gq_ref, gk_ref, gv_ref)):
-                ref[:, columns] = dot_tn(pick_buf[...], back_buf[head, which]).astype(BF16)
+                stage_buf[head, which] = dot_tn(pick_buf[...], back_buf[head, which]).astype(BF16)
+                pltpu.make_async_copy(
+                    stage_buf.at[head, which], ref.at[:, columns], store_sem.at[1 + which]
+                ).start()
         return carry
 
     lax.fori_loop(0, heads_dev, collect, 0)
@@ -444,6 +469,39 @@
 
     lax.fori_loop(0, heads_dev, drain, 0)
     wait_bytes(cot_buf.at[pl.ds(0, (n_sp - 1) * tok), :], csend_sem)
+    for which in range(4):
+        wait_bytes(oback_buf, store_sem.at[which])
+
+
+def place_kernel(*refs):
+    sources, targets, sems = refs[:4], refs[4:8], refs[8]
+    rows = 32
+    copies = []
+    for which in range(4):
+        for piece in range(sources[which].shape[0] // rows):
+            part = pl.ds(piece * rows, rows)
+            copies.append(
+                pltpu.make_async_copy(
+                    sources[which].at[part, :], targets[which].at[part, :], sems.at[len(copies)]
+                )
+            )
+            copies[-1].start()
+    for copy in copies:
+        copy.wait()
+
+
+def place_outputs(results):
+    hbm = pl.BlockSpec(memory_space=pltpu.HBM)
+    pieces = sum(result.shape[0] // 32 for result in results)
+    return pl.pallas_call(
+        place_kernel,
+        out_shape=[jax.ShapeDtypeStruct(result.shape, BF16) for result in results],
+        in_specs=[hbm] * 4,
+        out_specs=[hbm] * 4,
+        scratch_shapes=[pltpu.SemaphoreType.DMA((pieces,))],
+        compiler_params=pltpu.CompilerParams(vmem_limit_bytes=VMEM_GRANT),
+        name="place_outputs",
+    )(*results)
 
 
 def fused(
@@ -465,13 +523,15 @@
     group_tok = tok * n_sp
     smem = pl.BlockSpec(memory_space=pltpu.SMEM)
     vmem = pl.BlockSpec(memory_space=pltpu.VMEM)
+    hbm = pl.BlockSpec(memory_space=pltpu.HBM)
     flops = 2 * 8 * heads_dev * group_tok * group_tok * HD
     return pl.pallas_call(
         functools.partial(fused_kernel, n_dp, n_sp, tok // n, heads_dev),
         out_shape=[jax.ShapeDtypeStruct((tok, row_width), BF16)] * 4,
-        in_specs=[smem] * 4 + [vmem] * 5,
-        out_specs=[vmem] * 4,
+        in_specs=[smem] * 4 + [vmem] + [hbm] * 4,
+        out_specs=[hbm] * 4,
         scratch_shapes=[
+            pltpu.VMEM((heads_dev, n_sp, 3, tok, HD), BF16),
             pltpu.VMEM((HEADS, 3, tok, HD), BF16),
             pltpu.VMEM((heads_dev, 3, group_tok, HD), BF16),
             pltpu.VMEM((group_tok, heads_dev * HD), BF16),
@@ -482,6 +542,8 @@
             pltpu.VMEM((group_tok, group_tok), BF16),
             pltpu.VMEM((group_tok, group_tok), BF16),
             pltpu.VMEM((tok, tok), BF16),
+            pltpu.VMEM((HEADS, 3, tok, HD), BF16),
+            pltpu.SemaphoreType.DMA((heads_dev,)),
             pltpu.SemaphoreType.DMA((heads_dev,)),
             pltpu.SemaphoreType.DMA((heads_dev,)),
             pltpu.SemaphoreType.DMA((heads_dev,)),
@@ -491,9 +553,10 @@
             pltpu.SemaphoreType.DMA((heads_dev,)),
             pltpu.SemaphoreType.DMA((heads_dev,)),
             pltpu.SemaphoreType.DMA((3 * heads_dev + 1,)),
+            pltpu.SemaphoreType.DMA((4,)),
         ],
         compiler_params=pltpu.CompilerParams(
-            collective_id=0, has_side_effects=True, vmem_limit_bytes=48 * 1024 * 1024
+            collective_id=0, has_side_effects=True, vmem_limit_bytes=VMEM_GRANT
         ),
         cost_estimate=pl.CostEstimate(
             flops=flops, bytes_accessed=16 * tok * row_width, transcendentals=0
@@ -517,7 +580,7 @@
     tok = arrays[0].shape[0]
     block_rows = tok // (n_dp * n_sp)
     if (n_sp * block_rows) % 16 == 0 and HEADS % n_sp == 0:
-        return fused(n_dp, n_sp, *arrays)
+        return place_outputs(fused(n_dp, n_sp, *arrays))
     return per_device(*arrays)
 
 

time: 105 us -> 177 us (1.69)
  Pallas kernels: 94.5 us -> 176 us
  local copies, waits for them, and re-layouts: 9.73 us -> 0 us
    pallas_call x0 -> x1, Pallas kernels: none -> 80.7 us  [place_outputs(): pl.pallas_call(place_kernel, out_shape=[jax.ShapeDtypeStruct(result.shape...]
    unnamed x22 -> x0, local copies, waits for them, and re-layouts: 9.73 us -> none
where the time goes in v2:
time: 177 us; the launch traced here: 176 us
  Pallas kernels  176 us (99%)
    pallas_call x1, Pallas kernels, fused(): pl.pallas_call(functools.partial(fused_kernel, n_dp, n_sp, tok // n, head...  95 us
    pallas_call x1, Pallas kernels, place_outputs(): pl.pallas_call(place_kernel, out_shape=[jax.ShapeDtypeStruct(result.shape...  80.7 us

profile of v2, /device:TPU:0, one launch (start us, length us, event | category | flops | bytes accessed | tf_op | source)
XLA Modules:
  0.0 176.3 jit_solution(9974502380852364268)
XLA Ops:
  0.6 95.0 %routed_attention.1 = (bf16[128,2560]{1,0:T(8,128)(2,1)}, bf16[128,2560]{1,0:T(8,128)(2,1)}, bf16[128,2560]{1,0:T(8,128)(2,1)}, bf16[128,2560]{1,0:T(8,128)(2,1)}) custom-call(s32[8]{0:T(128)} %length_ref.1, s32[8]{0:T(128)} %plan_ref.1, s32[8]{0:T(128)} %bin_ref.1, f32[8,20]{1,0:T(8,128)} %table_ref.1, s32[8,128]{1,0:T(8,128)} %bitcast.1, ...), custom_call_target="tpu_custom_call" | custom-call | flops 2684354560 | bytes 5242880 | tf_op jit(solution)/shard_map/routed_attention/pallas_call | solution.py:528
  95.7 80.7 %place_outputs.1 = (bf16[128,2560]{1,0:T(8,128)(2,1)}, bf16[128,2560]{1,0:T(8,128)(2,1)}, bf16[128,2560]{1,0:T(8,128)(2,1)}, bf16[128,2560]{1,0:T(8,128)(2,1)}) custom-call(bf16[128,2560]{1,0:T(8,128)(2,1)} %get-tuple-element.8.refs_0_, bf16[128,2560]{1,0:T(8,128)(2,1)} %get-tuple-element.9.refs_1_, bf16[128,2560]{1,0:T(8,128)(2,1)} %get-tuple-element.10.refs_2_, ...), custom_call_target="tpu_custom_call" | custom-call | tf_op jit(solution)/shard_map/place_outputs/pallas_call | solution.py:496

commit v3 on v2

--- a/solution.py
+++ b/solution.py
@@ -221,12 +221,9 @@
     tok = q_ref.shape[0]
     group_tok = tok * n_sp
     group_blocks = group_tok // block_rows
-    others = (n - 1) * chunk
     group = lax.axis_index("dp")
     part = lax.axis_index("sp")
     me = group * n_sp + part
-    my_rows = pl.ds(pl.multiple_of(me * chunk, chunk), chunk)
-    my_group_rows = pl.ds(pl.multiple_of(group * chunk, chunk), chunk)
     my_part_rows = pl.ds(pl.multiple_of(part * tok, tok), tok)
 
     def load(j, carry):
@@ -271,9 +268,11 @@
         for part_to in range(n_sp):
             head = part_to * heads_dev + j
             for which in range(3):
-                send_buf[head, which] = dot_nn(
-                    pick_buf[...], load_buf[j, part_to, which]
-                ).astype(BF16)
+                send_buf[head, :, which] = (
+                    dot_nn(pick_buf[...], load_buf[j, part_to, which])
+                    .astype(BF16)
+                    .reshape(n_dp, chunk, HD)
+                )
 
     def peer_at(i):
         turn = i + (i + n - 3) // (n - 1)
@@ -286,13 +285,8 @@
         def one(i, carry):
             to_group, to_part = peer_at(i)
             pltpu.make_async_remote_copy(
-                src_ref=send_buf.at[
-                    to_part * heads_dev + j,
-                    :,
-                    pl.ds(pl.multiple_of(to_group * chunk, chunk), chunk),
-                    :,
-                ],
-                dst_ref=recv_buf.at[j, :, my_rows, :],
+                src_ref=send_buf.at[to_part * heads_dev + j, to_group],
+                dst_ref=recv_buf.at[j, me],
                 send_sem=send_sem.at[j],
                 recv_sem=recv_sem.at[j],
                 device_id=(to_group, to_part),
@@ -302,8 +296,8 @@
 
         lax.fori_loop(0, n - 1, one, 0)
         pltpu.make_async_copy(
-            send_buf.at[part * heads_dev + j, :, my_group_rows, :],
-            recv_buf.at[j, :, my_rows, :],
+            send_buf.at[part * heads_dev + j, group],
+            recv_buf.at[j, me],
             local_sem.at[j],
         ).start()
 
@@ -312,8 +306,8 @@
             to_group, to_part = peer_at(i)
             to = to_group * n_sp + to_part
             pltpu.make_async_remote_copy(
-                src_ref=grad_buf.at[j, :, pl.ds(pl.multiple_of(to * chunk, chunk), chunk), :],
-                dst_ref=back_buf.at[part * heads_dev + j, :, my_group_rows, :],
+                src_ref=grad_buf.at[j, to],
+                dst_ref=back_buf.at[part * heads_dev + j, group],
                 send_sem=gsend_sem.at[j],
                 recv_sem=back_sem.at[j],
                 device_id=(to_group, to_part),
@@ -323,8 +317,8 @@
 
         lax.fori_loop(0, n - 1, one, 0)
         pltpu.make_async_copy(
-            grad_buf.at[j, :, my_rows, :],
-            back_buf.at[part * heads_dev + j, :, my_group_rows, :],
+            grad_buf.at[j, me],
+            back_buf.at[part * heads_dev + j, group],
             local_sem.at[heads_dev + j],
         ).start()
 
@@ -417,9 +411,9 @@
         gate = table_ref[group_bin, part * heads_dev + j]
         columns = pl.ds(pl.multiple_of(j * HD, HD), HD)
         d_out = (gate * dot_nn(order_buf[...], cot_buf[:, columns])).astype(BF16)
-        wait_bytes(recv_buf.at[j, :, pl.ds(0, others), :], recv_sem.at[j])
-        wait_bytes(recv_buf.at[j, :, my_rows, :], local_sem.at[j])
-        query, key, value = recv_buf[j, 0], recv_buf[j, 1], recv_buf[j, 2]
+        wait_bytes(recv_buf.at[j, pl.ds(0, n - 1)], recv_sem.at[j])
+        wait_bytes(recv_buf.at[j, me], local_sem.at[j])
+        query, key, value = (recv_buf[j, :, at].reshape(group_tok, HD) for at in range(3))
         scores = dot_nt(key, query) * scale
         scores = jnp.where(key_live > 0.5, scores, -1e30)
         top = jnp.max(scores, axis=0, keepdims=True)
@@ -430,9 +424,9 @@
         grad_attend = dot_nt(value, d_out)
         row_dot = jnp.sum(attend_bf.astype(F32) * grad_attend, axis=0, keepdims=True)
         grad_scores = (attend * (grad_attend - row_dot) * scale).astype(BF16)
-        grad_buf[j, 2] = dot_nn(attend_bf, d_out).astype(BF16)
-        grad_buf[j, 1] = dot_nn(grad_scores, query).astype(BF16)
-        grad_buf[j, 0] = dot_tn(grad_scores, key).astype(BF16)
+        grad_buf[j, :, 2] = dot_nn(attend_bf, d_out).astype(BF16).reshape(n, chunk, HD)
+        grad_buf[j, :, 1] = dot_nn(grad_scores, query).astype(BF16).reshape(n, chunk, HD)
+        grad_buf[j, :, 0] = dot_tn(grad_scores, key).astype(BF16).reshape(n, chunk, HD)
         output = dot_tn(attend_bf, value).astype(BF16)
         gated = (gate * output.astype(F32)).astype(BF16)
         out_buf[j] = dot_nn(unorder_buf[...], gated).astype(BF16)
@@ -442,8 +436,8 @@
     lax.fori_loop(0, heads_dev, one_head, 0)
 
     def collect(j, carry):
-        wait_bytes(recv_buf.at[j, :, pl.ds(0, others), :], back_sem.at[j])
-        wait_bytes(recv_buf.at[j, :, my_rows, :], local_sem.at[heads_dev + j])
+        wait_bytes(recv_buf.at[j, pl.ds(0, n - 1)], back_sem.at[j])
+        wait_bytes(recv_buf.at[j, me], local_sem.at[heads_dev + j])
         wait_bytes(out_buf.at[j, pl.ds(0, (n_sp - 1) * tok), :], orecv_sem.at[j])
         wait_bytes(out_buf.at[j, my_part_rows, :], local_sem.at[2 * heads_dev + j])
         for part_from in range(n_sp):
@@ -453,7 +447,8 @@
                 oback_buf.at[head], out_ref.at[:, columns], store_sem.at[0]
             ).start()
             for which, ref in enumerate((gq_ref, gk_ref, gv_ref)):
-                stage_buf[head, which] = dot_tn(pick_buf[...], back_buf[head, which]).astype(BF16)
+                arrived = back_buf[head, :, which].reshape(n_dp * chunk, HD)
+                stage_buf[head, which] = dot_tn(pick_buf[...], arrived).astype(BF16)
                 pltpu.make_async_copy(
                     stage_buf.at[head, which], ref.at[:, columns], store_sem.at[1 + which]
                 ).start()
@@ -462,8 +457,8 @@
     lax.fori_loop(0, heads_dev, collect, 0)
 
     def drain(j, carry):
-        wait_bytes(recv_buf.at[j, :, pl.ds(0, others), :], send_sem.at[j])
-        wait_bytes(recv_buf.at[j, :, pl.ds(0, others), :], gsend_sem.at[j])
+        wait_bytes(recv_buf.at[j, pl.ds(0, n - 1)], send_sem.at[j])
+        wait_bytes(recv_buf.at[j, pl.ds(0, n - 1)], gsend_sem.at[j])
         wait_bytes(out_buf.at[j, pl.ds(0, (n_sp - 1) * tok), :], osend_sem.at[j])
         return carry
 
@@ -474,31 +469,45 @@
 
 
 def place_kernel(*refs):
-    sources, targets, sems = refs[:4], refs[4:8], refs[8]
+    sources, targets, held, in_sems, out_sems = refs[:4], refs[4:8], refs[8], refs[9], refs[10]
     rows = 32
-    copies = []
-    for which in range(4):
-        for piece in range(sources[which].shape[0] // rows):
-            part = pl.ds(piece * rows, rows)
-            copies.append(
-                pltpu.make_async_copy(
-                    sources[which].at[part, :], targets[which].at[part, :], sems.at[len(copies)]
-                )
-            )
-            copies[-1].start()
-    for copy in copies:
-        copy.wait()
+    pieces = sources[0].shape[0] // rows
+
+    def copies_of(which, piece):
+        at = pl.ds(piece * rows, rows)
+        index = which * pieces + piece
+        return (
+            pltpu.make_async_copy(
+                sources[which].at[at, :], held.at[which, at, :], in_sems.at[index]
+            ),
+            pltpu.make_async_copy(
+                held.at[which, at, :], targets[which].at[at, :], out_sems.at[index]
+            ),
+        )
+
+    pairs = [copies_of(which, piece) for which in range(4) for piece in range(pieces)]
+    for inward, _ in pairs:
+        inward.start()
+    for inward, outward in pairs:
+        inward.wait()
+        outward.start()
+    for _, outward in pairs:
+        outward.wait()
 
 
 def place_outputs(results):
     hbm = pl.BlockSpec(memory_space=pltpu.HBM)
-    pieces = sum(result.shape[0] // 32 for result in results)
+    pieces = 4 * (results[0].shape[0] // 32)
     return pl.pallas_call(
         place_kernel,
         out_shape=[jax.ShapeDtypeStruct(result.shape, BF16) for result in results],
         in_specs=[hbm] * 4,
         out_specs=[hbm] * 4,
-        scratch_shapes=[pltpu.SemaphoreType.DMA((pieces,))],
+        scratch_shapes=[
+            pltpu.VMEM((4,) + results[0].shape, BF16),
+            pltpu.SemaphoreType.DMA((pieces,)),
+            pltpu.SemaphoreType.DMA((pieces,)),
+        ],
         compiler_params=pltpu.CompilerParams(vmem_limit_bytes=VMEM_GRANT),
         name="place_outputs",
     )(*results)
@@ -532,11 +541,11 @@
         out_specs=[hbm] * 4,
         scratch_shapes=[
             pltpu.VMEM((heads_dev, n_sp, 3, tok, HD), BF16),
-            pltpu.VMEM((HEADS, 3, tok, HD), BF16),
-            pltpu.VMEM((heads_dev, 3, group_tok, HD), BF16),
+            pltpu.VMEM((HEADS, n_dp, 3, tok // n_dp, HD), BF16),
+            pltpu.VMEM((heads_dev, n, 3, group_tok // n, HD), BF16),
             pltpu.VMEM((group_tok, heads_dev * HD), BF16),
-            pltpu.VMEM((heads_dev, 3, group_tok, HD), BF16),
-            pltpu.VMEM((HEADS, 3, tok, HD), BF16),
+            pltpu.VMEM((heads_dev, n, 3, group_tok // n, HD), BF16),
+            pltpu.VMEM((HEADS, n_dp, 3, tok // n_dp, HD), BF16),
             pltpu.VMEM((heads_dev, group_tok, HD), BF16),
             pltpu.VMEM((HEADS, tok, HD), BF16),
             pltpu.VMEM((group_tok, group_tok), BF16),

time: 177 us -> 98.7 us (0.56)
  Pallas kernels: 176 us -> 97.8 us
    pallas_call x1, Pallas kernels: 80.7 us -> 2.78 us  [place_outputs(): pl.pallas_call(place_kernel, out_shape=[jax.ShapeDtypeStruct(result.shape...]
where the time goes in v3:
time: 98.7 us; the launch traced here: 98.4 us
  Pallas kernels  97.8 us (99%)
    pallas_call x1, Pallas kernels, fused(): pl.pallas_call(functools.partial(fused_kernel, n_dp, n_sp, tok // n, head...  95 us
    pallas_call x1, Pallas kernels, place_outputs(): pl.pallas_call(place_kernel, out_shape=[jax.ShapeDtypeStruct(result.shape...  2.78 us

profile of v3, /device:TPU:0, one launch (start us, length us, event | category | flops | bytes accessed | tf_op | source)
XLA Modules:
  0.0 98.4 jit_solution(1378151832284716875)
XLA Ops:
  0.6 95.0 %routed_attention.1 = (bf16[128,2560]{1,0:T(8,128)(2,1)}, bf16[128,2560]{1,0:T(8,128)(2,1)}, bf16[128,2560]{1,0:T(8,128)(2,1)}, bf16[128,2560]{1,0:T(8,128)(2,1)}) custom-call(s32[8]{0:T(128)} %length_ref.1, s32[8]{0:T(128)} %plan_ref.1, s32[8]{0:T(128)} %bin_ref.1, f32[8,20]{1,0:T(8,128)} %table_ref.1, s32[8,128]{1,0:T(8,128)} %bitcast.1, ...), custom_call_target="tpu_custom_call" | custom-call | flops 2684354560 | bytes 5242880 | tf_op jit(solution)/shard_map/routed_attention/pallas_call | solution.py:537
  95.7 2.8 %place_outputs.1 = (bf16[128,2560]{1,0:T(8,128)(2,1)}, bf16[128,2560]{1,0:T(8,128)(2,1)}, bf16[128,2560]{1,0:T(8,128)(2,1)}, bf16[128,2560]{1,0:T(8,128)(2,1)}) custom-call(bf16[128,2560]{1,0:T(8,128)(2,1)} %get-tuple-element.8.refs_0_, bf16[128,2560]{1,0:T(8,128)(2,1)} %get-tuple-element.9.refs_1_, bf16[128,2560]{1,0:T(8,128)(2,1)} %get-tuple-element.10.refs_2_, ...), custom_call_target="tpu_custom_call" | custom-call | tf_op jit(solution)/shard_map/place_outputs/pallas_call | solution.py:501

commit v4 on v3

--- a/solution.py
+++ b/solution.py
@@ -281,14 +281,14 @@
         peer = outer * quarter + (me % quarter + turn // 4) % quarter
         return peer // n_sp, peer % n_sp
 
-    def forward(j):
+    def forward(at, first, size):
         def one(i, carry):
             to_group, to_part = peer_at(i)
             pltpu.make_async_remote_copy(
-                src_ref=send_buf.at[to_part * heads_dev + j, to_group],
-                dst_ref=recv_buf.at[j, me],
-                send_sem=send_sem.at[j],
-                recv_sem=recv_sem.at[j],
+                src_ref=send_buf.at[pl.ds(to_part * heads_dev + first, size), to_group],
+                dst_ref=recv_buf.at[pl.ds(first, size), me],
+                send_sem=send_sem.at[at],
+                recv_sem=recv_sem.at[at],
                 device_id=(to_group, to_part),
                 device_id_type=MESH,
             ).start()
@@ -296,20 +296,20 @@
 
         lax.fori_loop(0, n - 1, one, 0)
         pltpu.make_async_copy(
-            send_buf.at[part * heads_dev + j, group],
-            recv_buf.at[j, me],
-            local_sem.at[j],
+            send_buf.at[pl.ds(part * heads_dev + first, size), group],
+            recv_buf.at[pl.ds(first, size), me],
+            local_sem.at[at],
         ).start()
 
-    def backward(j):
+    def backward(at, first, size):
         def one(i, carry):
             to_group, to_part = peer_at(i)
             to = to_group * n_sp + to_part
             pltpu.make_async_remote_copy(
-                src_ref=grad_buf.at[j, to],
-                dst_ref=back_buf.at[part * heads_dev + j, group],
-                send_sem=gsend_sem.at[j],
-                recv_sem=back_sem.at[j],
+                src_ref=grad_buf.at[pl.ds(first, size), to],
+                dst_ref=back_buf.at[pl.ds(part * heads_dev + first, size), group],
+                send_sem=gsend_sem.at[at],
+                recv_sem=back_sem.at[at],
                 device_id=(to_group, to_part),
                 device_id_type=MESH,
             ).start()
@@ -317,31 +317,44 @@
 
         lax.fori_loop(0, n - 1, one, 0)
         pltpu.make_async_copy(
-            grad_buf.at[j, me],
-            back_buf.at[part * heads_dev + j, group],
-            local_sem.at[heads_dev + j],
+            grad_buf.at[pl.ds(first, size), me],
+            back_buf.at[pl.ds(part * heads_dev + first, size), group],
+            local_sem.at[heads_dev + at],
         ).start()
 
         for step in range(1, n_sp):
             to_part = (part + step) % n_sp
             pltpu.make_async_remote_copy(
-                src_ref=out_buf.at[j, pl.ds(pl.multiple_of(to_part * tok, tok), tok), :],
-                dst_ref=oback_buf.at[part * heads_dev + j],
-                send_sem=osend_sem.at[j],
-                recv_sem=orecv_sem.at[j],
+                src_ref=out_buf.at[
+                    pl.ds(first, size), pl.ds(pl.multiple_of(to_part * tok, tok), tok), :
+                ],
+                dst_ref=oback_buf.at[pl.ds(part * heads_dev + first, size)],
+                send_sem=osend_sem.at[at],
+                recv_sem=orecv_sem.at[at],
                 device_id=(group, to_part),
                 device_id_type=MESH,
             ).start()
         pltpu.make_async_copy(
-            out_buf.at[j, my_part_rows, :],
-            oback_buf.at[part * heads_dev + j],
-            local_sem.at[2 * heads_dev + j],
+            out_buf.at[pl.ds(first, size), my_part_rows, :],
+            oback_buf.at[pl.ds(part * heads_dev + first, size)],
+            local_sem.at[2 * heads_dev + at],
         ).start()
 
     width = heads_dev * HD
-    prepare(0)
+    batches = [
+        (at, first, min(2, heads_dev - first)) for at, first in enumerate(range(0, heads_dev, 2))
+    ]
+
+    def prepare_batch(first, size):
+        def one(j, carry):
+            prepare(j)
+            return carry
+
+        lax.fori_loop(first, first + size, one, 0)
+
+    prepare_batch(0, batches[0][2])
     pl.semaphore_wait(barrier, n - 1)
-    forward(0)
+    forward(*batches[0])
     for step in range(1, n_sp):
         to_part = (part + step) % n_sp
         pltpu.make_async_remote_copy(
@@ -358,12 +371,9 @@
         local_sem.at[3 * heads_dev],
     ).start()
 
-    def send_more(j, carry):
-        prepare(j)
-        forward(j)
-        return carry
-
-    lax.fori_loop(1, heads_dev, send_more, 0)
+    for at, first, size in batches[1:]:
+        prepare_batch(first, size)
+        forward(at, first, size)
 
     group_len = jnp.int32(0)
     group_bin = jnp.int32(0)
@@ -411,8 +421,14 @@
         gate = table_ref[group_bin, part * heads_dev + j]
         columns = pl.ds(pl.multiple_of(j * HD, HD), HD)
         d_out = (gate * dot_nn(order_buf[...], cot_buf[:, columns])).astype(BF16)
-        wait_bytes(recv_buf.at[j, pl.ds(0, n - 1)], recv_sem.at[j])
-        wait_bytes(recv_buf.at[j, me], local_sem.at[j])
+        for at, first, size in batches:
+
+            @pl.when(j == first)
+            def _():
+                heads = pl.ds(first, size)
+                wait_bytes(recv_buf.at[heads, pl.ds(0, n - 1)], recv_sem.at[at])
+                wait_bytes(recv_buf.at[heads, me], local_sem.at[at])
+
         query, key, value = (recv_buf[j, :, at].reshape(group_tok, HD) for at in range(3))
         scores = dot_nt(key, query) * scale
         scores = jnp.where(key_live > 0.5, scores, -1e30)
@@ -430,16 +446,27 @@
         output = dot_tn(attend_bf, value).astype(BF16)
         gated = (gate * output.astype(F32)).astype(BF16)
         out_buf[j] = dot_nn(unorder_buf[...], gated).astype(BF16)
-        backward(j)
+        for at, first, size in batches:
+
+            @pl.when(j == first + size - 1)
+            def _():
+                backward(at, first, size)
+
         return carry
 
     lax.fori_loop(0, heads_dev, one_head, 0)
 
     def collect(j, carry):
-        wait_bytes(recv_buf.at[j, pl.ds(0, n - 1)], back_sem.at[j])
-        wait_bytes(recv_buf.at[j, me], local_sem.at[heads_dev + j])
-        wait_bytes(out_buf.at[j, pl.ds(0, (n_sp - 1) * tok), :], orecv_sem.at[j])
-        wait_bytes(out_buf.at[j, my_part_rows, :], local_sem.at[2 * heads_dev + j])
+        for at, first, size in batches:
+
+            @pl.when(j == first)
+            def _():
+                heads = pl.ds(first, size)
+                wait_bytes(recv_buf.at[heads, pl.ds(0, n - 1)], back_sem.at[at])
+                wait_bytes(recv_buf.at[heads, me], local_sem.at[heads_dev + at])
+                wait_bytes(out_buf.at[heads, pl.ds(0, (n_sp - 1) * tok), :], orecv_sem.at[at])
+                wait_bytes(out_buf.at[heads, my_part_rows, :], local_sem.at[2 * heads_dev + at])
+
         for part_from in range(n_sp):
             head = part_from * heads_dev + j
             columns = pl.ds(pl.multiple_of(head * HD, HD), HD)
@@ -456,13 +483,11 @@
 
     lax.fori_loop(0, heads_dev, collect, 0)
 
-    def drain(j, carry):
-        wait_bytes(recv_buf.at[j, pl.ds(0, n - 1)], send_sem.at[j])
-        wait_bytes(recv_buf.at[j, pl.ds(0, n - 1)], gsend_sem.at[j])
-        wait_bytes(out_buf.at[j, pl.ds(0, (n_sp - 1) * tok), :], osend_sem.at[j])
-        return carry
-
-    lax.fori_loop(0, heads_dev, drain, 0)
+    for at, first, size in batches:
+        heads = pl.ds(first, size)
+        wait_bytes(recv_buf.at[heads, pl.ds(0, n - 1)], send_sem.at[at])
+        wait_bytes(recv_buf.at[heads, pl.ds(0, n - 1)], gsend_sem.at[at])
+        wait_bytes(out_buf.at[heads, pl.ds(0, (n_sp - 1) * tok), :], osend_sem.at[at])
     wait_bytes(cot_buf.at[pl.ds(0, (n_sp - 1) * tok), :], csend_sem)
     for which in range(4):
         wait_bytes(oback_buf, store_sem.at[which])

time: 98.7 us -> 98.8 us (level)
  no operation moved by 1% of the time
where the time goes in v4:
time: 98.8 us; the launch traced here: 98.4 us
  Pallas kernels  97.8 us (99%)
    pallas_call x1, Pallas kernels, fused(): pl.pallas_call(functools.partial(fused_kernel, n_dp, n_sp, tok // n, head...  95 us
    pallas_call x1, Pallas kernels, place_outputs(): pl.pallas_call(place_kernel, out_shape=[jax.ShapeDtypeStruct(result.shape...  2.78 us

profile of v4, /device:TPU:0, one launch (start us, length us, event | category | flops | bytes accessed | tf_op | source)
XLA Modules:
  0.0 98.4 jit_solution(16596053805347401423)
XLA Ops:
  0.6 95.0 %routed_attention.1 = (bf16[128,2560]{1,0:T(8,128)(2,1)}, bf16[128,2560]{1,0:T(8,128)(2,1)}, bf16[128,2560]{1,0:T(8,128)(2,1)}, bf16[128,2560]{1,0:T(8,128)(2,1)}) custom-call(s32[8]{0:T(128)} %length_ref.1, s32[8]{0:T(128)} %plan_ref.1, s32[8]{0:T(128)} %bin_ref.1, f32[8,20]{1,0:T(8,128)} %table_ref.1, s32[8,128]{1,0:T(8,128)} %bitcast.1, ...), custom_call_target="tpu_custom_call" | custom-call | flops 2684354560 | bytes 5242880 | tf_op jit(solution)/shard_map/routed_attention/pallas_call | solution.py:562
  95.7 2.8 %place_outputs.1 = (bf16[128,2560]{1,0:T(8,128)(2,1)}, bf16[128,2560]{1,0:T(8,128)(2,1)}, bf16[128,2560]{1,0:T(8,128)(2,1)}, bf16[128,2560]{1,0:T(8,128)(2,1)}) custom-call(bf16[128,2560]{1,0:T(8,128)(2,1)} %get-tuple-element.8.refs_0_, bf16[128,2560]{1,0:T(8,128)(2,1)} %get-tuple-element.9.refs_1_, bf16[128,2560]{1,0:T(8,128)(2,1)} %get-tuple-element.10.refs_2_, ...), custom_call_target="tpu_custom_call" | custom-call | tf_op jit(solution)/shard_map/place_outputs/pallas_call | solution.py:526

commit v5 on v4

--- a/solution.py
+++ b/solution.py
@@ -10,7 +10,7 @@
 HEADS = 20
 HD = 128
 MESH = pl.DeviceIdType.MESH
-VMEM_GRANT = 62 * 1024 * 1024
+VMEM_GRANT = 48 * 1024 * 1024
 F32 = jnp.float32
 BF16 = jnp.bfloat16
 
@@ -203,7 +203,6 @@
     order_buf,
     unorder_buf,
     pick_buf,
-    stage_buf,
     load_sem,
     send_sem,
     recv_sem,
@@ -214,7 +213,6 @@
     osend_sem,
     orecv_sem,
     local_sem,
-    store_sem,
 ):
     n = n_dp * n_sp
     chunk = n_sp * block_rows
@@ -226,6 +224,10 @@
     me = group * n_sp + part
     my_part_rows = pl.ds(pl.multiple_of(part * tok, tok), tok)
 
+    batches = [
+        (at, first, min(2, heads_dev - first)) for at, first in enumerate(range(0, heads_dev, 2))
+    ]
+
     def load(j, carry):
         for part_to in range(n_sp):
             columns = pl.ds(pl.multiple_of((part_to * heads_dev + j) * HD, HD), HD)
@@ -246,7 +248,7 @@
         return carry
 
     lax.fori_loop(0, n - 1, greet, 0)
-    lax.fori_loop(1, heads_dev, load, 0)
+    lax.fori_loop(1, batches[0][2], load, 0)
 
     source = source_ref[...]
     loader_of = source // n
@@ -341,10 +343,6 @@
         ).start()
 
     width = heads_dev * HD
-    batches = [
-        (at, first, min(2, heads_dev - first)) for at, first in enumerate(range(0, heads_dev, 2))
-    ]
-
     def prepare_batch(first, size):
         def one(j, carry):
             prepare(j)
@@ -355,6 +353,7 @@
     prepare_batch(0, batches[0][2])
     pl.semaphore_wait(barrier, n - 1)
     forward(*batches[0])
+    lax.fori_loop(batches[0][2], heads_dev, load, 0)
     for step in range(1, n_sp):
         to_part = (part + step) % n_sp
         pltpu.make_async_remote_copy(
@@ -470,15 +469,10 @@
         for part_from in range(n_sp):
             head = part_from * heads_dev + j
             columns = pl.ds(pl.multiple_of(head * HD, HD), HD)
-            pltpu.make_async_copy(
-                oback_buf.at[head], out_ref.at[:, columns], store_sem.at[0]
-            ).start()
+            out_ref[:, columns] = oback_buf[head]
             for which, ref in enumerate((gq_ref, gk_ref, gv_ref)):
                 arrived = back_buf[head, :, which].reshape(n_dp * chunk, HD)
-                stage_buf[head, which] = dot_tn(pick_buf[...], arrived).astype(BF16)
-                pltpu.make_async_copy(
-                    stage_buf.at[head, which], ref.at[:, columns], store_sem.at[1 + which]
-                ).start()
+                ref[:, columns] = dot_tn(pick_buf[...], arrived).astype(BF16)
         return carry
 
     lax.fori_loop(0, heads_dev, collect, 0)
@@ -489,51 +483,34 @@
         wait_bytes(recv_buf.at[heads, pl.ds(0, n - 1)], gsend_sem.at[at])
         wait_bytes(out_buf.at[heads, pl.ds(0, (n_sp - 1) * tok), :], osend_sem.at[at])
     wait_bytes(cot_buf.at[pl.ds(0, (n_sp - 1) * tok), :], csend_sem)
-    for which in range(4):
-        wait_bytes(oback_buf, store_sem.at[which])
 
 
 def place_kernel(*refs):
-    sources, targets, held, in_sems, out_sems = refs[:4], refs[4:8], refs[8], refs[9], refs[10]
+    sources, targets, sems = refs[:4], refs[4:8], refs[8]
     rows = 32
     pieces = sources[0].shape[0] // rows
-
-    def copies_of(which, piece):
-        at = pl.ds(piece * rows, rows)
-        index = which * pieces + piece
-        return (
-            pltpu.make_async_copy(
-                sources[which].at[at, :], held.at[which, at, :], in_sems.at[index]
-            ),
-            pltpu.make_async_copy(
-                held.at[which, at, :], targets[which].at[at, :], out_sems.at[index]
-            ),
-        )
-
-    pairs = [copies_of(which, piece) for which in range(4) for piece in range(pieces)]
-    for inward, _ in pairs:
-        inward.start()
-    for inward, outward in pairs:
-        inward.wait()
-        outward.start()
-    for _, outward in pairs:
-        outward.wait()
+    copies = []
+    for which in range(4):
+        for piece in range(pieces):
+            at = pl.ds(piece * rows, rows)
+            copies.append(
+                pltpu.make_async_copy(
+                    sources[which].at[at, :], targets[which].at[at, :], sems.at[len(copies)]
+                )
+            )
+            copies[-1].start()
+    for copy in copies:
+        copy.wait()
 
 
 def place_outputs(results):
-    hbm = pl.BlockSpec(memory_space=pltpu.HBM)
-    pieces = 4 * (results[0].shape[0] // 32)
     return pl.pallas_call(
         place_kernel,
         out_shape=[jax.ShapeDtypeStruct(result.shape, BF16) for result in results],
-        in_specs=[hbm] * 4,
-        out_specs=[hbm] * 4,
-        scratch_shapes=[
-            pltpu.VMEM((4,) + results[0].shape, BF16),
-            pltpu.SemaphoreType.DMA((pieces,)),
-            pltpu.SemaphoreType.DMA((pieces,)),
-        ],
-        compiler_params=pltpu.CompilerParams(vmem_limit_bytes=VMEM_GRANT),
+        in_specs=[pl.BlockSpec(memory_space=pltpu.VMEM)] * 4,
+        out_specs=[pl.BlockSpec(memory_space=pltpu.HBM)] * 4,
+        scratch_shapes=[pltpu.SemaphoreType.DMA((4 * (results[0].shape[0] // 32),))],
+        compiler_params=pltpu.CompilerParams(vmem_limit_bytes=16 * 1024 * 1024),
         name="place_outputs",
     )(*results)
 
@@ -563,7 +540,7 @@
         functools.partial(fused_kernel, n_dp, n_sp, tok // n, heads_dev),
         out_shape=[jax.ShapeDtypeStruct((tok, row_width), BF16)] * 4,
         in_specs=[smem] * 4 + [vmem] + [hbm] * 4,
-        out_specs=[hbm] * 4,
+        out_specs=[vmem] * 4,
         scratch_shapes=[
             pltpu.VMEM((heads_dev, n_sp, 3, tok, HD), BF16),
             pltpu.VMEM((HEADS, n_dp, 3, tok // n_dp, HD), BF16),
@@ -576,7 +553,6 @@
             pltpu.VMEM((group_tok, group_tok), BF16),
             pltpu.VMEM((group_tok, group_tok), BF16),
             pltpu.VMEM((tok, tok), BF16),
-            pltpu.VMEM((HEADS, 3, tok, HD), BF16),
             pltpu.SemaphoreType.DMA((heads_dev,)),
             pltpu.SemaphoreType.DMA((heads_dev,)),
             pltpu.SemaphoreType.DMA((heads_dev,)),
@@ -587,7 +563,6 @@
             pltpu.SemaphoreType.DMA((heads_dev,)),
             pltpu.SemaphoreType.DMA((heads_dev,)),
             pltpu.SemaphoreType.DMA((3 * heads_dev + 1,)),
-            pltpu.SemaphoreType.DMA((4,)),
         ],
         compiler_params=pltpu.CompilerParams(
             collective_id=0, has_side_effects=True, vmem_limit_bytes=VMEM_GRANT
@@ -597,15 +572,20 @@
         ),
         name="routed_attention",
     )(
-        lengths,
-        sample_plan,
-        guide_bins,
-        guide_table,
-        block_source.reshape(n_dp, block_source.shape[0] // n_dp),
-        queries,
-        key_rows,
-        value_rows,
-        cotangent,
+        *(
+            pltpu.with_memory_space_constraint(array, pltpu.HBM)
+            for array in (
+                lengths,
+                sample_plan,
+                guide_bins,
+                guide_table,
+                block_source.reshape(n_dp, block_source.shape[0] // n_dp),
+                queries,
+                key_rows,
+                value_rows,
+                cotangent,
+            )
+        ),
     )
 
 

time: 98.8 us -> 96.8 us (0.980)
  Pallas kernels: 97.8 us -> 95.9 us
    pallas_call x1, Pallas kernels: 2.78 us -> 1.62 us  [place_outputs(): pl.pallas_call(place_kernel, out_shape=[jax.ShapeDtypeStruct(result.shape...]
where the time goes in v5:
time: 96.8 us; the launch traced here: 96.5 us
  Pallas kernels  95.9 us (99%)
    pallas_call x1, Pallas kernels, fused(): pl.pallas_call(functools.partial(fused_kernel, n_dp, n_sp, tok // n, head...  94.3 us

profile of v5, /device:TPU:0, one launch (start us, length us, event | category | flops | bytes accessed | tf_op | source)
XLA Modules:
  0.0 96.5 jit_solution(10117304979390102958)
XLA Ops:
  0.6 94.3 %routed_attention.1 = (bf16[128,2560]{1,0:T(8,128)(2,1)S(1)}, bf16[128,2560]{1,0:T(8,128)(2,1)S(1)}, bf16[128,2560]{1,0:T(8,128)(2,1)S(1)}, bf16[128,2560]{1,0:T(8,128)(2,1)S(1)}) custom-call(s32[8]{0:T(128)} %length_ref.1, s32[8]{0:T(128)} %plan_ref.1, s32[8]{0:T(128)} %bin_ref.1, f32[8,20]{1,0:T(8,128)} %table_ref.1, s32[8,128]{1,0:T(8,128)} %bitcast.1, ...), custom_call_target="tpu_custom_call" | custom-call | flops 2684354560 | bytes 5242880 | tf_op jit(solution)/shard_map/routed_attention/pallas_call | solution.py:539
  94.9 1.6 %place_outputs.1 = (bf16[128,2560]{1,0:T(8,128)(2,1)}, bf16[128,2560]{1,0:T(8,128)(2,1)}, bf16[128,2560]{1,0:T(8,128)(2,1)}, bf16[128,2560]{1,0:T(8,128)(2,1)}) custom-call(bf16[128,2560]{1,0:T(8,128)(2,1)S(1)} %get-tuple-element.8.refs_0_, bf16[128,2560]{1,0:T(8,128)(2,1)S(1)} %get-tuple-element.9.refs_1_, bf16[128,2560]{1,0:T(8,128)(2,1)S(1)} %get-tuple-element.10.refs_2_, ...), custom_call_target="tpu_custom_call" | custom-call | tf_op jit(solution)/shard_map/place_outputs/pallas_call | solution.py:507

commit v6 on v5

--- a/solution.py
+++ b/solution.py
@@ -224,8 +224,10 @@
     me = group * n_sp + part
     my_part_rows = pl.ds(pl.multiple_of(part * tok, tok), tok)
 
+    starts = [0] + list(range(1, heads_dev - 2, 2)) + [heads_dev - 2, heads_dev - 1]
     batches = [
-        (at, first, min(2, heads_dev - first)) for at, first in enumerate(range(0, heads_dev, 2))
+        (at, first, last - first)
+        for at, (first, last) in enumerate(zip(starts, starts[1:] + [heads_dev]))
     ]
 
     def load(j, carry):
@@ -238,7 +240,6 @@
         return carry
 
     barrier = pltpu.get_barrier_semaphore()
-    load(0, 0)
 
     def greet(i, carry):
         peer = (me + 1 + i) % n
@@ -248,7 +249,7 @@
         return carry
 
     lax.fori_loop(0, n - 1, greet, 0)
-    lax.fori_loop(1, batches[0][2], load, 0)
+    load(0, 0)
 
     source = source_ref[...]
     loader_of = source // n

time: 96.8 us -> 96.8 us (level)
  no operation moved by 1% of the time
where the time goes in v6:
time: 96.8 us; the launch traced here: 96.5 us
  Pallas kernels  95.9 us (99%)
    pallas_call x1, Pallas kernels, fused(): pl.pallas_call(functools.partial(fused_kernel, n_dp, n_sp, tok // n, head...  94.3 us

profile of v6, /device:TPU:0, one launch (start us, length us, event | category | flops | bytes accessed | tf_op | source)
XLA Modules:
  0.0 96.5 jit_solution(5536071621906813988)
XLA Ops:
  0.6 94.3 %routed_attention.1 = (bf16[128,2560]{1,0:T(8,128)(2,1)S(1)}, bf16[128,2560]{1,0:T(8,128)(2,1)S(1)}, bf16[128,2560]{1,0:T(8,128)(2,1)S(1)}, bf16[128,2560]{1,0:T(8,128)(2,1)S(1)}) custom-call(s32[8]{0:T(128)} %length_ref.1, s32[8]{0:T(128)} %plan_ref.1, s32[8]{0:T(128)} %bin_ref.1, f32[8,20]{1,0:T(8,128)} %table_ref.1, s32[8,128]{1,0:T(8,128)} %bitcast.1, ...), custom_call_target="tpu_custom_call" | custom-call | flops 2684354560 | bytes 5242880 | tf_op jit(solution)/shard_map/routed_attention/pallas_call | solution.py:540
  94.9 1.6 %place_outputs.1 = (bf16[128,2560]{1,0:T(8,128)(2,1)}, bf16[128,2560]{1,0:T(8,128)(2,1)}, bf16[128,2560]{1,0:T(8,128)(2,1)}, bf16[128,2560]{1,0:T(8,128)(2,1)}) custom-call(bf16[128,2560]{1,0:T(8,128)(2,1)S(1)} %get-tuple-element.8.refs_0_, bf16[128,2560]{1,0:T(8,128)(2,1)S(1)} %get-tuple-element.9.refs_1_, bf16[128,2560]{1,0:T(8,128)(2,1)S(1)} %get-tuple-element.10.refs_2_, ...), custom_call_target="tpu_custom_call" | custom-call | tf_op jit(solution)/shard_map/place_outputs/pallas_call | solution.py:508
